TPU v7x, 32 devices: a whole 2x2x4 slice. The times are simulated.
32 devices in a mesh: dp: 8 (over z, x), tensor: 4 (over y, core).
Axes of the slice: x: 2, y: 2, z: 4, core: 2. Of those that a mesh axis runs over, the one named last changes fastest.
Arguments:
- tokens: bfloat16 [8192, 1024], P(('dp', 'tensor')), may hold values from -6 to 6
- cotangent: bfloat16 [8192, 1024], P(('dp', 'tensor')), may hold values from -6 to 6
- document_index: int32 [8, 1024], P('dp'), may hold values from 0 to 3, as said below
- routes: int32 [8192, 8], P('dp'), may hold values from 0 to 31, all different within a row; in each aligned block of 1024 rows (0 to 1023, 1024 to 2047, ...) at most 512 rows name the same one
- gain_attn: bfloat16 [1024], P(('dp', 'tensor')), may hold values from 0.5 to 1.5
- gain_moe: bfloat16 [1024], P(('dp', 'tensor')), may hold values from 0.5 to 1.5
- w_query: bfloat16 [1024, 1024], P('dp', 'tensor'), may hold values from -0.1875 to 0.1875
- key_weight: bfloat16 [1024, 512], P('dp', 'tensor'), may hold values from -0.1875 to 0.1875
- value_weight: bfloat16 [1024, 512], P('dp', 'tensor'), may hold values from -0.1875 to 0.1875
- w_out: bfloat16 [1024, 1024], P('dp', 'tensor'), may hold values from -0.75 to 0.75
- w_router: bfloat16 [1024, 32], P(('dp', 'tensor')), may hold values from -0.08984375 to 0.08984375
- w_gate: bfloat16 [1024, 32, 512], P('dp', None, 'tensor'), may hold values from -0.1875 to 0.1875
- w_up: bfloat16 [1024, 32, 512], P('dp', None, 'tensor'), may hold values from -0.1875 to 0.1875
- w_down: bfloat16 [1024, 32, 512], P('dp', None, 'tensor'), may hold values from -1 to 1
Outputs:
- output: bfloat16 [8192, 1024], P(('dp', 'tensor'))
- grad_tokens: bfloat16 [8192, 1024], P(('dp', 'tensor'))
- grad_gain_attn: float32 [1024], P(('dp', 'tensor'))
- grad_gain_moe: float32 [1024], P(('dp', 'tensor'))
- grad_query: float32 [1024, 1024], P('dp', 'tensor')
- grad_key: float32 [1024, 512], P('dp', 'tensor')
- grad_value: float32 [1024, 512], P('dp', 'tensor')
- grad_out: float32 [1024, 1024], P('dp', 'tensor')
- grad_router: float32 [1024, 32], P(('dp', 'tensor'))
- grad_gate: float32 [1024, 32, 512], P('dp', None, 'tensor')
- grad_up: float32 [1024, 32, 512], P('dp', None, 'tensor')
- grad_down: float32 [1024, 32, 512], P('dp', None, 'tensor')
Inputs may be any that keep to these rules, and one draw needn't show every extreme that they name: `document_index`: along each sequence the numbers start at 0 and never fall; a sequence holds exactly 4 documents of 200 tokens or more each, and the last token has number 4 - 1. `routes`: each row names 8 different experts. In each aligned block of 1024 rows (the tokens of one index of dp) no expert is named by more than 512 rows, a bound that some block reaches.
All inputs are finite; a program needn't handle non-finite values.
Results may differ from a plain program's by a relative error of at most 0.023.
Values may be sent and summed in bfloat16 or wider, within the bound.
A program may use at most 320 MiB of HBM per device.

v0:
```python
import jax
import jax.numpy as jnp
from jax import lax
from jax.sharding import PartitionSpec as P

HEAD_SIZE = 64
CAP = 512


eps_norm = 1e-06
rope_base = 10000.0


def plain_dot(left, right):
    return jnp.dot(left, right, preferred_element_type=jnp.float32)


def dot_right_t(left, right):
    return lax.dot_general(
        left, right, (((1,), (1,)), ((), ())), preferred_element_type=jnp.float32
    )


def dot_left_t(left, right):
    return lax.dot_general(
        left, right, (((0,), (0,)), ((), ())), preferred_element_type=jnp.float32
    )


def doc_positions(segment_row):
    places = jnp.arange(segment_row.shape[0], dtype=jnp.int32)
    before = jnp.sum((segment_row[None, :] < segment_row[:, None]).astype(jnp.int32), axis=1)
    return places - before


def rotate_pairs(field, token_positions, heads, sign):
    length_tokens = field.shape[0]
    half = HEAD_SIZE // 2
    freqs = rope_base ** (-2.0 * jnp.arange(half, dtype=jnp.float32) / HEAD_SIZE)
    angles = token_positions.astype(jnp.float32)[:, None] * freqs[None, :]
    cosine = jnp.cos(angles)[:, None, :]
    sine = sign * jnp.sin(angles)[:, None, :]
    shaped = field.reshape(length_tokens, heads, HEAD_SIZE)
    first = shaped[:, :, :half]
    second = shaped[:, :, half:]
    turned = jnp.concatenate(
        [first * cosine - second * sine, second * cosine + first * sine], axis=2
    )
    return turned.reshape(length_tokens, heads * HEAD_SIZE)


def norm_backward(field, inverse, gain, upstream):
    scaled = upstream * gain
    gain_grad = jnp.sum(upstream * field * inverse, axis=0)
    inner = jnp.mean(scaled * field, axis=1, keepdims=True)
    return (inverse * scaled - field * inverse**3 * inner, gain_grad)


def body(
    tokens,
    cotangent,
    document_index,
    routes,
    gain_attn,
    gain_moe,
    w_query,
    key_weight,
    value_weight,
    w_out,
    w_router,
    w_gate,
    w_up,
    w_down,
):
    parts = lax.axis_size("tensor")
    local_rows = tokens.shape[0]
    group_rows = local_rows * parts
    width = tokens.shape[1]
    sequences = document_index.shape[0]
    length_tokens = document_index.shape[1]
    my_index = lax.axis_index("tensor")
    experts = w_gate.shape[1]
    top = routes.shape[1]
    scale = HEAD_SIZE ** (-0.5)
    gain_one, gain_two, router_full = (
        lax.all_gather(gain_attn, ("dp", "tensor"), axis=0, tiled=True),
        lax.all_gather(gain_moe, ("dp", "tensor"), axis=0, tiled=True),
        lax.all_gather(w_router, ("dp", "tensor"), axis=0, tiled=True),
    )
    gain_one_f = gain_one.astype(jnp.float32)
    gain_two_f = gain_two.astype(jnp.float32)
    full_query, full_key, full_value, full_out, full_gate, full_up, full_down = (
        lax.all_gather(w_query, "dp", axis=0, tiled=True),
        lax.all_gather(key_weight, "dp", axis=0, tiled=True),
        lax.all_gather(value_weight, "dp", axis=0, tiled=True),
        lax.all_gather(w_out, "dp", axis=0, tiled=True),
        lax.all_gather(w_gate, "dp", axis=0, tiled=True),
        lax.all_gather(w_up, "dp", axis=0, tiled=True),
        lax.all_gather(w_down, "dp", axis=0, tiled=True),
    )
    tokens_f = tokens.astype(jnp.float32)
    inverse_one = lax.rsqrt(jnp.mean(tokens_f * tokens_f, axis=1, keepdims=True) + eps_norm)
    normed_one = (tokens_f * inverse_one * gain_one_f).astype(jnp.bfloat16)
    normed_all = lax.all_gather(normed_one, "tensor", axis=0, tiled=True)
    q_width = full_query.shape[1]
    kv_width = full_key.shape[1]
    heads_q = q_width // HEAD_SIZE
    heads_kv = kv_width // HEAD_SIZE
    query_group = heads_q // heads_kv
    joined = jnp.concatenate([full_query, full_key, full_value], axis=1)
    projected = plain_dot(normed_all, joined)
    token_positions = jax.vmap(doc_positions)(document_index).reshape(-1)
    query_b = rotate_pairs(projected[:, :q_width], token_positions, heads_q, 1.0).astype(
        jnp.bfloat16
    )
    key_b = rotate_pairs(
        projected[:, q_width : q_width + kv_width], token_positions, heads_kv, 1.0
    ).astype(jnp.bfloat16)
    value_b = projected[:, q_width + kv_width :].astype(jnp.bfloat16)

    def scores_of(query_s, key_s, segment_s):
        heads_of_query = query_s.reshape(length_tokens, heads_kv, query_group, HEAD_SIZE)
        heads_of_key = key_s.reshape(length_tokens, heads_kv, HEAD_SIZE)
        raw = (
            jnp.einsum(
                "qkgd,skd->kgqs", heads_of_query, heads_of_key, preferred_element_type=jnp.float32
            )
            * scale
        )
        places = jnp.arange(length_tokens, dtype=jnp.int32)
        allowed = (segment_s[None, :] == segment_s[:, None]) & (places[None, :] <= places[:, None])
        return jnp.where(allowed[None, None], raw, -1e30)

    def forward_one(packed):
        query_s, key_s, value_s, segment_s = packed
        masked = scores_of(query_s, key_s, segment_s)
        peak = jnp.max(masked, axis=-1, keepdims=True)
        weights = jnp.exp(masked - peak)
        total = jnp.sum(weights, axis=-1, keepdims=True)
        probs = (weights / total).astype(jnp.bfloat16)
        heads_of_value = value_s.reshape(length_tokens, heads_kv, HEAD_SIZE)
        mixed = jnp.einsum(
            "kgqs,skd->qkgd", probs, heads_of_value, preferred_element_type=jnp.float32
        )
        return (mixed.reshape(length_tokens, q_width).astype(jnp.bfloat16), peak + jnp.log(total))

    query_seq = query_b.reshape(sequences, length_tokens, q_width)
    key_seq = key_b.reshape(sequences, length_tokens, kv_width)
    value_seq = value_b.reshape(sequences, length_tokens, kv_width)
    attended_rows, log_totals = lax.map(
        forward_one, (query_seq, key_seq, value_seq, document_index)
    )
    attended_all = attended_rows.reshape(group_rows, q_width)
    piece = attended_all
    middle = tokens_f + lax.psum_scatter(
        dot_right_t(piece, full_out).astype(jnp.bfloat16), "tensor", scatter_dimension=0, tiled=True
    ).astype(jnp.float32)
    inverse_two = lax.rsqrt(jnp.mean(middle * middle, axis=1, keepdims=True) + eps_norm)
    normed_two = (middle * inverse_two * gain_two_f).astype(jnp.bfloat16)
    logits = plain_dot(normed_two, router_full)
    expert_ids = jnp.arange(experts, dtype=jnp.int32)
    local_routes = lax.dynamic_slice_in_dim(routes, my_index * local_rows, local_rows, 0)
    chosen = (local_routes[:, :, None] == expert_ids[None, None, :]).astype(jnp.float32)
    picked = jnp.sum(chosen * logits[:, None, :], axis=2)
    picked_peak = jnp.max(picked, axis=1, keepdims=True)
    picked_exp = jnp.exp(picked - picked_peak)
    gates_f = picked_exp / jnp.sum(picked_exp, axis=1, keepdims=True)
    normed_two_all, gates_all = (
        lax.all_gather(normed_two, "tensor", axis=0, tiled=True),
        lax.all_gather(gates_f.astype(jnp.bfloat16), "tensor", axis=0, tiled=True),
    )
    gates_all_f = gates_all.astype(jnp.float32)
    flattened = routes.reshape(-1)
    order = jnp.argsort(flattened, stable=True)
    counts = jnp.sum((flattened[:, None] == expert_ids[None, :]).astype(jnp.int32), axis=0)
    starts = jnp.cumsum(counts) - counts
    slots = jnp.arange(CAP, dtype=jnp.int32)
    table = order[jnp.minimum(starts[:, None] + slots[None, :], flattened.shape[0] - 1)]
    filled = (slots[None, :] < counts[:, None]).astype(jnp.float32)
    token_of = table // top
    route_of = table % top
    token_flat = token_of.reshape(-1)
    slot_weight = gates_all_f[token_of, route_of] * filled
    inputs_disp = normed_two_all[token_of]
    gate_kept = jnp.einsum(
        "ecd,def->ecf", inputs_disp, full_gate, preferred_element_type=jnp.float32
    )
    up_kept = jnp.einsum("ecd,def->ecf", inputs_disp, full_up, preferred_element_type=jnp.float32)
    active_fwd = (jax.nn.silu(gate_kept) * up_kept).astype(jnp.bfloat16)
    result_disp = jnp.einsum(
        "ecf,def->ecd", active_fwd, full_down, preferred_element_type=jnp.float32
    )
    weighted = (slot_weight[:, :, None] * result_disp).reshape(-1, width)
    moe_all = jnp.zeros((group_rows, width), jnp.float32).at[token_flat].add(weighted)
    moe_local = lax.psum_scatter(
        moe_all.astype(jnp.bfloat16), "tensor", scatter_dimension=0, tiled=True
    ).astype(jnp.float32)
    output = (middle + moe_local).astype(jnp.bfloat16)
    upstream = cotangent.astype(jnp.float32)
    moe_grads_all = lax.all_gather(cotangent, "tensor", axis=0, tiled=True)
    grads_disp = moe_grads_all[token_of]
    sigma = jax.nn.sigmoid(gate_kept)
    swish = gate_kept * sigma
    folded = jnp.einsum("ecd,def->ecf", grads_disp, full_down, preferred_element_type=jnp.float32)
    gate_grad_slot = jnp.sum(active_fwd.astype(jnp.float32) * folded, axis=2) * filled
    scaled = (slot_weight[:, :, None] * grads_disp.astype(jnp.float32)).astype(jnp.bfloat16)
    active_grad = jnp.einsum("ecd,def->ecf", scaled, full_down, preferred_element_type=jnp.float32)
    down_local = jnp.einsum("ecd,ecf->def", scaled, active_fwd, preferred_element_type=jnp.float32)
    gate_pre_grad = (active_grad * up_kept * sigma * (1.0 + gate_kept * (1.0 - sigma))).astype(
        jnp.bfloat16
    )
    up_pre_grad = (active_grad * swish).astype(jnp.bfloat16)
    gate_local = jnp.einsum(
        "ecd,ecf->def", inputs_disp, gate_pre_grad, preferred_element_type=jnp.float32
    )
    up_local = jnp.einsum(
        "ecd,ecf->def", inputs_disp, up_pre_grad, preferred_element_type=jnp.float32
    )
    input_grad = jnp.einsum(
        "ecf,def->ecd", gate_pre_grad, full_gate, preferred_element_type=jnp.float32
    ) + jnp.einsum("ecf,def->ecd", up_pre_grad, full_up, preferred_element_type=jnp.float32)
    rows_grad_all = (
        jnp.zeros((group_rows, width), jnp.float32)
        .at[token_flat]
        .add(input_grad.reshape(-1, width))
    )
    gates_grad_all = (
        jnp.zeros((group_rows, top), jnp.float32).at[token_of, route_of].add(gate_grad_slot)
    )
    normed_two_grad, gates_grad = (
        lax.psum_scatter(
            rows_grad_all.astype(jnp.bfloat16), "tensor", scatter_dimension=0, tiled=True
        ).astype(jnp.float32),
        lax.psum_scatter(
            gates_grad_all.astype(jnp.bfloat16), "tensor", scatter_dimension=0, tiled=True
        ).astype(jnp.float32),
    )
    inner = jnp.sum(gates_f * gates_grad, axis=1, keepdims=True)
    picked_grad = gates_f * (gates_grad - inner)
    logits_grad = jnp.sum(chosen * picked_grad[:, :, None], axis=1).astype(jnp.bfloat16)
    router_grad = dot_left_t(normed_two, logits_grad)
    normed_two_grad = normed_two_grad + dot_right_t(logits_grad, router_full)
    middle_part, gain_two_grad = norm_backward(middle, inverse_two, gain_two_f, normed_two_grad)
    middle_grad = upstream + middle_part
    piece = lax.all_gather(middle_grad.astype(jnp.bfloat16), "tensor", axis=0, tiled=True)
    mixed_grad = plain_dot(piece, full_out)
    out_weight_grad = dot_left_t(piece, attended_all)
    attended_grad_b = mixed_grad.astype(jnp.bfloat16).reshape(sequences, length_tokens, q_width)

    def backward_one(packed):
        query_s, key_s, value_s, segment_s, log_total, grad_s = packed
        masked = scores_of(query_s, key_s, segment_s)
        probs_f = jnp.exp(masked - log_total)
        probs = probs_f.astype(jnp.bfloat16)
        heads_of_query = query_s.reshape(length_tokens, heads_kv, query_group, HEAD_SIZE)
        heads_of_key = key_s.reshape(length_tokens, heads_kv, HEAD_SIZE)
        heads_of_value = value_s.reshape(length_tokens, heads_kv, HEAD_SIZE)
        grad_heads = grad_s.reshape(length_tokens, heads_kv, query_group, HEAD_SIZE)
        prob_grad = jnp.einsum(
            "qkgd,skd->kgqs", grad_heads, heads_of_value, preferred_element_type=jnp.float32
        )
        row_inner = jnp.sum(probs_f * prob_grad, axis=-1, keepdims=True)
        score_grad = (probs_f * (prob_grad - row_inner)).astype(jnp.bfloat16)
        query_grad = (
            jnp.einsum(
                "kgqs,skd->qkgd", score_grad, heads_of_key, preferred_element_type=jnp.float32
            )
            * scale
        )
        key_grad = (
            jnp.einsum(
                "kgqs,qkgd->skd", score_grad, heads_of_query, preferred_element_type=jnp.float32
            )
            * scale
        )
        value_grad = jnp.einsum(
            "kgqs,qkgd->skd", probs, grad_heads, preferred_element_type=jnp.float32
        )
        return (
            query_grad.reshape(length_tokens, q_width),
            key_grad.reshape(length_tokens, kv_width),
            value_grad.reshape(length_tokens, kv_width),
        )

    query_grad, key_grad, value_grad = lax.map(
        backward_one, (query_seq, key_seq, value_seq, document_index, log_totals, attended_grad_b)
    )
    query_pre_grad = rotate_pairs(
        query_grad.reshape(group_rows, q_width), token_positions, heads_q, -1.0
    ).astype(jnp.bfloat16)
    key_pre_grad = rotate_pairs(
        key_grad.reshape(group_rows, kv_width), token_positions, heads_kv, -1.0
    ).astype(jnp.bfloat16)
    value_pre_grad = value_grad.reshape(group_rows, kv_width).astype(jnp.bfloat16)
    joined_grad = jnp.concatenate([query_pre_grad, key_pre_grad, value_pre_grad], axis=1)
    joined_weight_grad = dot_left_t(normed_all, joined_grad)
    piece = joined_grad
    normed_one_grad = lax.psum_scatter(
        dot_right_t(piece, joined).astype(jnp.bfloat16), "tensor", scatter_dimension=0, tiled=True
    ).astype(jnp.float32)
    tokens_part, gain_one_grad = norm_backward(tokens_f, inverse_one, gain_one_f, normed_one_grad)
    grad_tokens = (middle_grad + tokens_part).astype(jnp.bfloat16)
    grad_query, grad_key, grad_value, grad_out, grad_gate, grad_up, grad_down = (
        lax.psum_scatter(joined_weight_grad[:, :q_width], "dp", scatter_dimension=0, tiled=True),
        lax.psum_scatter(
            joined_weight_grad[:, q_width : q_width + kv_width],
            "dp",
            scatter_dimension=0,
            tiled=True,
        ),
        lax.psum_scatter(
            joined_weight_grad[:, q_width + kv_width :], "dp", scatter_dimension=0, tiled=True
        ),
        lax.psum_scatter(out_weight_grad, "dp", scatter_dimension=0, tiled=True),
        lax.psum_scatter(gate_local, "dp", scatter_dimension=0, tiled=True),
        lax.psum_scatter(up_local, "dp", scatter_dimension=0, tiled=True),
        lax.psum_scatter(down_local, "dp", scatter_dimension=0, tiled=True),
    )
    grad_gain_attn, grad_gain_moe, grad_router = (
        lax.psum_scatter(gain_one_grad, ("dp", "tensor"), scatter_dimension=0, tiled=True),
        lax.psum_scatter(gain_two_grad, ("dp", "tensor"), scatter_dimension=0, tiled=True),
        lax.psum_scatter(router_grad, ("dp", "tensor"), scatter_dimension=0, tiled=True),
    )
    return (
        output,
        grad_tokens,
        grad_gain_attn,
        grad_gain_moe,
        grad_query,
        grad_key,
        grad_value,
        grad_out,
        grad_router,
        grad_gate,
        grad_up,
        grad_down,
    )


def solution(mesh):
    return jax.shard_map(
        body,
        mesh=mesh,
        in_specs=(
            P(("dp", "tensor"), None),
            P(("dp", "tensor"), None),
            P("dp", None),
            P("dp", None),
            P(("dp", "tensor")),
            P(("dp", "tensor")),
            P("dp", "tensor"),
            P("dp", "tensor"),
            P("dp", "tensor"),
            P("dp", "tensor"),
            P(("dp", "tensor"), None),
            P("dp", None, "tensor"),
            P("dp", None, "tensor"),
            P("dp", None, "tensor"),
        ),
        out_specs=(
            P(("dp", "tensor"), None),
            P(("dp", "tensor"), None),
            P(("dp", "tensor")),
            P(("dp", "tensor")),
            P("dp", "tensor"),
            P("dp", "tensor"),
            P("dp", "tensor"),
            P("dp", "tensor"),
            P(("dp", "tensor"), None),
            P("dp", None, "tensor"),
            P("dp", None, "tensor"),
            P("dp", None, "tensor"),
        ),
        check_vma=False,
    )
```

profile of v0, /device:TPU:0, one launch (start us, length us, event | category | flops | bytes accessed | tf_op | source)
XLA Modules:
  0.0 2630.5 jit_solution(9924164859709341026)
XLA Ops:
  10.7 42.0 %all-reduce.5 = (bf16[1024]{0:T(1024)(128)(2,1)S(1)}, bf16[1024]{0:T(1024)(128)(2,1)S(1)}) all-reduce(bf16[1024]{0:T(1024)(128)(2,1)S(1)} %dynamic-update-slice, bf16[1024]{0:T(1024)(128)(2,1)S(1)} %dynamic-update-slice.1), channel_id=1, replica_groups=mesh['dp'=8,'tensor'=4] {'dp','tensor'}, use_global_device_ids=true, to_apply=%add | all-reduce | flops 2048 | bytes 8192
  55.5 31.0 %all_gather.48 = bf16[1024,128]{1,0:T(8,128)(2,1)S(1)} all-gather(bf16[128,128]{1,0:T(8,128)(2,1)} %param.21), channel_id=1, replica_groups=mesh['dp'=8,'tensor'=4] {'dp'}, dimensions={0}, use_global_device_ids=true | all-gather | bytes 294912 | tf_op jit(solution)/shard_map/all_gather | solution.py:94
  86.5 31.0 %all_gather.49 = bf16[1024,128]{1,0:T(8,128)(2,1)S(1)} all-gather(bf16[128,128]{1,0:T(8,128)(2,1)} %param.22), channel_id=1, replica_groups=mesh['dp'=8,'tensor'=4] {'dp'}, dimensions={0}, use_global_device_ids=true | all-gather | bytes 294912 | tf_op jit(solution)/shard_map/all_gather | solution.py:95
  117.5 31.4 %all_gather.47 = bf16[1024,256]{1,0:T(8,128)(2,1)S(1)} all-gather(bf16[128,256]{1,0:T(8,128)(2,1)} %param.20), channel_id=1, replica_groups=mesh['dp'=8,'tensor'=4] {'dp'}, dimensions={0}, use_global_device_ids=true | all-gather | bytes 589824 | tf_op jit(solution)/shard_map/all_gather | solution.py:93
  150.5 31.9 %all_gather.50 = bf16[1024,256]{1,0:T(8,128)(2,1)S(1)} all-gather(bf16[128,256]{1,0:T(8,128)(2,1)} %param.23), channel_id=1, replica_groups=mesh['dp'=8,'tensor'=4] {'dp'}, dimensions={0}, use_global_device_ids=true | all-gather | bytes 589824 | tf_op jit(solution)/shard_map/all_gather | solution.py:96
  215.1 30.7 %reduce-scatter.14.cloned.1.call-done = bf16[256,1024]{1,0:T(8,128)(2,1)} async-done(((bf16[1024,1024]{1,0:T(8,128)(2,1)}), bf16[256,1024]{1,0:T(8,128)(2,1)}) %reduce-scatter.14.cloned.1.call-update) | async-done | bytes 524304 | tf_op jit(solution)/shard_map/reduce_scatter | solution.py:155
  264.2 90.5 %gather_fusion = s32[16384]{0:T(1024)S(1)} fusion(s32[8192]{0:T(1024)S(1)} %get-tuple-element.54, s32[16384]{0:T(1024)S(1)} %broadcast_clamp_fusion.1), kind=kCustom, calls=%fused_computation | custom fusion | bytes 196608 | tf_op jit(solution)/shard_map/gather | solution.py:178
  355.7 42.7 %all_gather.52 = bf16[1024,32]{1,0:T(8,128)(2,1)S(1)} all-gather(bf16[32,32]{1,0:T(8,128)(2,1)S(1)} %copy-done.65), channel_id=1, replica_groups=mesh['dp'=8,'tensor'=4] {'dp','tensor'}, dimensions={0}, use_global_device_ids=true | all-gather | bytes 67584 | tf_op jit(solution)/shard_map/all_gather | solution.py:88
  399.5 82.0 %gather_fusion.3 = bf16[16384,1024]{1,0:T(8,128)(2,1)} fusion(bf16[1024,1024]{1,0:T(8,128)(2,1)} %all-gather.18.cloned.1.call-done, s32[16384]{0:T(1024)S(1)} %broadcast_clamp_fusion), kind=kCustom, calls=%fused_computation.3 | custom fusion | bytes 67174400 | tf_op jit(solution)/shard_map/gather | solution.py:201
  487.9 96.5 %gather_fusion.1 = f32[16384]{0:T(1024)S(1)} fusion(f32[1024,8]{0,1:T(8,128)S(1)} %convert_element_type.176, s32[16384]{0:T(1024)S(1)} %bitcast.127), kind=kCustom, calls=%fused_computation.1 | custom fusion | bytes 262144 | tf_op jit(solution)/shard_map/gather | solution.py:183
  584.4 82.0 %gather_fusion.2 = bf16[16384,1024]{1,0:T(8,128)(2,1)} fusion(bf16[1024,1024]{1,0:T(8,128)(2,1)} %all-gather.10.cloned.1.call-done, s32[16384]{0:T(1024)S(1)} %broadcast_clamp_fusion), kind=kCustom, calls=%fused_computation.2 | custom fusion | bytes 67174400 | tf_op jit(solution)/shard_map/gather | solution.py:184
  666.5 21.3 fusion.63
  687.8 21.4 fusion.62
  709.3 25.9 multiply_convert_fusion.5
  754.0 86.7 %scatter_custom_fusion.2 = f32[8192]{0:T(1024)S(1)} fusion(s32[16384]{0:T(1024)} %bitcast.162, f32[16384]{0:T(1024)S(1)} %bitcast.163, f32[]{:T(128)} %constant.112.clone.1), kind=kCustom, calls=%fused_computation.127 | custom fusion | flops 16384 | bytes 33280
  841.5 27.7 %fusion.64 = f32[32,512,1024]{2,1,0:T(8,128)} fusion(bf16[32,512,128]{1,2,0:T(8,128)(2,1)} %get-tuple-element.148, bf16[1024,32,128]{0,2,1:T(8,128)(2,1)} %all-gather.12.cloned.1.call-done), kind=kOutput, calls=%fused_computation.164 | convolution fusion | flops 4294967296 | bytes 79691776 | tf_op jit(solution)/shard_map/ecf,def->ecd/dot_general | solution.py:219
  869.2 46.6 %convolution_add_fusion = f32[32,512,1024]{2,1,0:T(8,128)} fusion(f32[32,512,1024]{2,1,0:T(8,128)} %fusion.64, bf16[32,512,128]{1,2,0:T(8,128)(2,1)} %get-tuple-element.147, bf16[1024,32,128]{0,2,1:T(8,128)(2,1)} %all-gather.14.cloned.1.call-done), kind=kOutput, calls=%fused_computation.11 | convolution fusion | flops 4311744512 | bytes 146800640 | tf_op jit(solution)/shard_map/ecf,def->ecd/dot_general | solution.py:221
  915.9 142.7 %scatter_custom_fusion.1 = f32[1024,1024]{1,0:T(8,128)} fusion(s32[16384]{0:T(1024)} %bitcast.160, f32[16384,1024]{1,0:T(8,128)} %bitcast.18, f32[]{:T(128)} %constant.112.clone.1), kind=kCustom, calls=%fused_computation.44 | custom fusion | flops 16777216 | bytes 4194816 | tf_op jit(solution)/shard_map/scatter-add | solution.py:225
  1064.2 29.7 %reduce-scatter.18.cloned.1.call-done = bf16[256,1024]{1,0:T(8,128)(2,1)} async-done(((bf16[1024,1024]{1,0:T(8,128)(2,1)}), bf16[256,1024]{1,0:T(8,128)(2,1)}) %reduce-scatter.18.cloned.1.call-update) | async-done | bytes 524304 | tf_op jit(solution)/shard_map/reduce_scatter | solution.py:231
  1098.6 22.6 all-gather.20.cloned.1.call-done
  1161.5 28.9 %broadcast_multiply_fusion = f32[32,512,1024]{2,1,0:T(8,128)} fusion(f32[32,512]{1,0:T(8,128)S(1)} %fusion.40, bf16[32,512,128]{1,2,0:T(8,128)(2,1)} %get-tuple-element.149, bf16[1024,32,128]{2,0,1:T(8,128)(2,1)} %all-gather.16.cloned.1.call-done), kind=kOutput, calls=%fused_computation.8 | convolution fusion | flops 4311744512 | bytes 79757312 | tf_op jit(solution)/shard_map/ecf,def->ecd/dot_general | solution.py:190
  1190.3 142.4 %scatter_custom_fusion = f32[1024,1024]{1,0:T(8,128)} fusion(s32[16384]{0:T(1024)} %bitcast.161, f32[16384,1024]{1,0:T(8,128)} %bitcast.16, f32[]{:T(128)} %constant.112.clone.1), kind=kCustom, calls=%fused_computation.46 | custom fusion | flops 16777216 | bytes 4194816 | tf_op jit(solution)/shard_map/scatter-add | solution.py:194
  1376.8 21.1 convolution_bitcast_fusion
  1413.7 43.8 %all-reduce.4 = (f32[1024]{0:T(1024)S(1)}, f32[1024]{0:T(1024)S(1)}) all-reduce(f32[1024]{0:T(1024)S(1)} %get-tuple-element.139, f32[1024]{0:T(1024)S(1)} %copy-done.54), channel_id=7, replica_groups=mesh['dp'=8,'tensor'=4] {'dp','tensor'}, use_global_device_ids=true, to_apply=%region_26.27.clone | all-reduce | flops 2048 | bytes 16384
  1461.7 194.8 %reduce-scatter.38.cloned.1.call-done = f32[128,32,128]{0,2,1:T(8,128)} async-done(((f32[1024,32,128]{0,2,1:T(8,128)}), f32[128,32,128]{0,2,1:T(8,128)}) %reduce-scatter.38.cloned.1.call-update) | async-done | bytes 2097168 | tf_op jit(solution)/shard_map/reduce_scatter | solution.py:317
  1659.5 282.4 %reduce-scatter.34.cloned.1.call-done = f32[128,32,128]{0,2,1:T(8,128)} async-done(((f32[1024,32,128]{0,2,1:T(8,128)}), f32[128,32,128]{0,2,1:T(8,128)}) %reduce-scatter.34.cloned.1.call-update) | async-done | bytes 2097168 | tf_op jit(solution)/shard_map/reduce_scatter | solution.py:315
  1944.9 282.9 %reduce-scatter.36.cloned.1.call-done = f32[128,32,128]{0,2,1:T(8,128)} async-done(((f32[1024,32,128]{0,2,1:T(8,128)}), f32[128,32,128]{0,2,1:T(8,128)}) %reduce-scatter.36.cloned.1.call-update) | async-done | bytes 2097168 | tf_op jit(solution)/shard_map/reduce_scatter | solution.py:316
  2230.9 132.6 %reduce-scatter.32.cloned.1.call-done = f32[32,32]{1,0:T(8,128)} async-done(((f32[1024,32]{1,0:T(8,128)}), f32[32,32]{1,0:T(8,128)}) %reduce-scatter.32.cloned.1.call-update) | async-done | bytes 4112 | tf_op jit(solution)/shard_map/reduce_scatter | solution.py:322
  2363.4 62.0 %reduce-scatter.28.cloned.1.call-done = f32[128,128]{1,0:T(8,128)} async-done(((f32[1024,128]{1,0:T(8,128)}), f32[128,128]{1,0:T(8,128)}) %reduce-scatter.28.cloned.1.call-update) | async-done | bytes 65552 | tf_op jit(solution)/shard_map/reduce_scatter | solution.py:311
  2425.5 64.8 %reduce-scatter.26.cloned.1.call-done = f32[128,128]{1,0:T(8,128)} async-done(((f32[1024,128]{1,0:T(8,128)}), f32[128,128]{1,0:T(8,128)}) %reduce-scatter.26.cloned.1.call-update) | async-done | bytes 65552 | tf_op jit(solution)/shard_map/reduce_scatter | solution.py:305
  2490.3 66.8 %reduce-scatter.30.cloned.1.call-done = f32[128,256]{1,0:T(8,128)} async-done(((f32[1024,256]{1,0:T(8,128)}), f32[128,256]{1,0:T(8,128)}) %reduce-scatter.30.cloned.1.call-update) | async-done | bytes 131088 | tf_op jit(solution)/shard_map/reduce_scatter | solution.py:314
  2557.0 66.4 %reduce-scatter.24.cloned.1.call-done = f32[128,256]{1,0:T(8,128)} async-done(((f32[1024,256]{1,0:T(8,128)}), f32[128,256]{1,0:T(8,128)}) %reduce-scatter.24.cloned.1.call-update) | async-done | bytes 131088 | tf_op jit(solution)/shard_map/reduce_scatter | solution.py:304
  (302 shorter events, 209.1 us)
Async XLA Ops:
  7.2 177.8 %all-gather.8.cloned.1.call-start = ((), (), s32[]{:S(2)}) async-start(), calls=%async_computation.13 | async-start | bytes 2621440 | tf_op jit(solution)/shard_map/all_gather | solution.py:104
  55.4 190.4 %reduce-scatter.14.cloned.1.call-start = ((), (), s32[]{:S(2)}) async-start(), calls=%async_computation.14 | async-start | bytes 2621440 | tf_op jit(solution)/shard_map/reduce_scatter | solution.py:155
  214.3 185.2 %all-gather.18.cloned.1.call-start = ((), (), s32[]{:S(2)}) async-start(), calls=%async_computation.20 | async-start | bytes 2621440 | tf_op jit(solution)/shard_map/all_gather | solution.py:200
  215.0 369.4 %all-gather.10.cloned.1.call-start = ((), (), s32[]{:S(2)}) async-start(), calls=%async_computation.15 | async-start | bytes 2621440 | tf_op jit(solution)/shard_map/all_gather | solution.py:169
  249.7 416.8 %all-gather.14.cloned.1.call-start = ((), (), s32[]{:S(2)}) async-start(), calls=%async_computation.17 | async-start | bytes 9437184 | tf_op jit(solution)/shard_map/all_gather | solution.py:98
  251.4 436.4 %all-gather.12.cloned.1.call-start = ((), (), s32[]{:S(2)}) async-start(), calls=%async_computation.16 | async-start | bytes 9437184 | tf_op jit(solution)/shard_map/all_gather | solution.py:97
  253.2 456.0 %all-gather.16.cloned.1.call-start = ((), (), s32[]{:S(2)}) async-start(), calls=%async_computation.18 | async-start | bytes 9437184 | tf_op jit(solution)/shard_map/all_gather | solution.py:99
  256.0 806.7 %reduce-scatter.20.cloned.1.call-start = ((), (), s32[]{:S(2)}) async-start(), calls=%async_computation.22 | async-start | bytes 20480 | tf_op jit(solution)/shard_map/reduce_scatter | solution.py:234
  263.7 320.6 %copy-start.63 = (s32[32]{0:T(128)}, s32[32]{0:T(128)S(1)}, u32[]{:S(2)}) copy-start(s32[32]{0:T(128)S(1)} %convert_reduce_fusion.1) | copy-start | bytes 388
  841.4 252.5 %reduce-scatter.18.cloned.1.call-start = ((), (), s32[]{:S(2)}) async-start(), calls=%async_computation.21 | async-start | bytes 2621440 | tf_op jit(solution)/shard_map/reduce_scatter | solution.py:231
  915.8 146.9 %copy-start.32 = (f32[256,8]{0,1:T(8,128)S(1)}, f32[256,8]{0,1:T(8,128)}, u32[]{:S(2)}) copy-start(f32[256,8]{0,1:T(8,128)} %copy-done.31) | copy-start | bytes 24580
  915.8 146.9 %copy-start.53 = (f32[256]{0:T(256)S(1)}, f32[256]{0:T(256)}, u32[]{:S(2)}) copy-start(f32[256]{0:T(256)} %copy-done.52) | copy-start | bytes 3076
  915.8 147.0 %copy-start.56 = (f32[256]{0:T(256)S(1)}, f32[256]{0:T(256)}, u32[]{:S(2)}) copy-start(f32[256]{0:T(256)} %copy-done.55) | copy-start | bytes 3076
  915.8 148.4 %copy-start.41 = (s32[256,8]{0,1:T(8,128)S(1)}, s32[256,8]{0,1:T(8,128)}, u32[]{:S(2)}) copy-start(s32[256,8]{0,1:T(8,128)} %copy-done.40) | copy-start | bytes 24580
  915.8 178.1 %copy-start.1 = (bf16[256,1024]{1,0:T(8,128)(2,1)S(1)}, bf16[256,1024]{1,0:T(8,128)(2,1)}, u32[]{:S(2)}) copy-start(bf16[256,1024]{1,0:T(8,128)(2,1)} %param.14) | copy-start | bytes 1572868
  915.8 178.1 %copy-start.3 = (bf16[256,1024]{1,0:T(8,128)(2,1)S(1)}, bf16[256,1024]{1,0:T(8,128)(2,1)}, u32[]{:S(2)}) copy-start(bf16[256,1024]{1,0:T(8,128)(2,1)} %reduce-scatter.14.cloned.1.call-done) | copy-start | bytes 1572868
  915.8 178.1 %copy-start.14 = (bf16[1024,32]{1,0:T(8,128)(2,1)S(1)}, bf16[1024,32]{1,0:T(8,128)(2,1)}, u32[]{:S(2)}) copy-start(bf16[1024,32]{1,0:T(8,128)(2,1)} %copy-done.13) | copy-start | bytes 196612
  915.9 178.1 %copy-start.38 = (f32[1024]{0:T(1024)S(1)}, f32[1024]{0:T(1024)}, u32[]{:S(2)}) copy-start(f32[1024]{0:T(1024)} %copy-done.37) | copy-start | bytes 12292
  915.9 178.1 %copy-start.50 = (f32[256]{0:T(256)S(1)}, f32[256]{0:T(256)}, u32[]{:S(2)}) copy-start(f32[256]{0:T(256)} %copy-done.49) | copy-start | bytes 3076
  915.9 181.4 %copy-start.9 = (bf16[256,1024]{1,0:T(8,128)(2,1)S(1)}, bf16[256,1024]{1,0:T(8,128)(2,1)}, u32[]{:S(2)}) copy-start(bf16[256,1024]{1,0:T(8,128)(2,1)} %param.15) | copy-start | bytes 1572868
  915.9 181.4 %copy-start.59 = (f32[256]{0:T(256)S(1)}, f32[256]{0:T(256)}, u32[]{:S(2)}) copy-start(f32[256]{0:T(256)} %get-tuple-element.168) | copy-start | bytes 3076
  1062.5 58.7 %all-gather.20.cloned.1.call-start = ((), (), s32[]{:S(2)}) async-start(), calls=%async_computation.23 | async-start | bytes 2621440 | tf_op jit(solution)/shard_map/all_gather | solution.py:245
  1098.5 313.8 %reduce-scatter.22.cloned.1.call-start = ((), (), s32[]{:S(2)}) async-start(), calls=%async_computation.24 | async-start | bytes 2621440 | tf_op jit(solution)/shard_map/reduce_scatter | solution.py:298
  1161.2 297.5 %reduce-scatter.16.cloned.1.call-start = ((), (), s32[]{:S(2)}) async-start(), calls=%async_computation.19 | async-start | bytes 2621440 | tf_op jit(solution)/shard_map/reduce_scatter | solution.py:195
  1336.6 319.8 %reduce-scatter.38.cloned.1.call-start = ((), (), s32[]{:S(2)}) async-start(), calls=%async_computation.32 | async-start | bytes 18874368 | tf_op jit(solution)/shard_map/reduce_scatter | solution.py:317
  1355.9 586.0 %reduce-scatter.34.cloned.1.call-start = ((), (), s32[]{:S(2)}) async-start(), calls=%async_computation.30 | async-start | bytes 18874368 | tf_op jit(solution)/shard_map/reduce_scatter | solution.py:315
  1376.5 851.3 %reduce-scatter.36.cloned.1.call-start = ((), (), s32[]{:S(2)}) async-start(), calls=%async_computation.31 | async-start | bytes 18874368 | tf_op jit(solution)/shard_map/reduce_scatter | solution.py:316
  1398.0 965.4 %reduce-scatter.32.cloned.1.call-start = ((), (), s32[]{:S(2)}) async-start(), calls=%async_computation.29 | async-start | bytes 540672 | tf_op jit(solution)/shard_map/reduce_scatter | solution.py:322
  1400.2 1025.2 %reduce-scatter.28.cloned.1.call-start = ((), (), s32[]{:S(2)}) async-start(), calls=%async_computation.27 | async-start | bytes 589824 | tf_op jit(solution)/shard_map/reduce_scatter | solution.py:311
  1405.7 1084.5 %reduce-scatter.26.cloned.1.call-start = ((), (), s32[]{:S(2)}) async-start(), calls=%async_computation.26 | async-start | bytes 589824 | tf_op jit(solution)/shard_map/reduce_scatter | solution.py:305
  1406.3 1150.7 %reduce-scatter.30.cloned.1.call-start = ((), (), s32[]{:S(2)}) async-start(), calls=%async_computation.28 | async-start | bytes 1179648 | tf_op jit(solution)/shard_map/reduce_scatter | solution.py:314
  1409.8 1213.7 %reduce-scatter.24.cloned.1.call-start = ((), (), s32[]{:S(2)}) async-start(), calls=%async_computation.25 | async-start | bytes 1179648 | tf_op jit(solution)/shard_map/reduce_scatter | solution.py:304
  (61 other events, 1879.2 us)
Sparse Core Ops, SparseCore 0:
  55.5 22.3 all-gather.7
  214.4 31.3 reduce-scatter.13
  247.4 22.6 all-gather.17
  272.1 22.6 all-gather.9
  297.4 127.5 all-gather.13
  427.7 122.8 all-gather.11
  552.9 123.0 all-gather.15
  841.6 19.1 reduce-scatter.19
  1062.6 31.2 reduce-scatter.17
  1098.6 22.5 all-gather.19
  1161.3 31.4 reduce-scatter.21
  1336.8 31.7 reduce-scatter.15
  1372.8 283.6 reduce-scatter.37
  1660.1 281.7 reduce-scatter.33
  1946.0 281.7 reduce-scatter.35
  2230.5 132.8 reduce-scatter.31
  2367.6 57.8 reduce-scatter.27
  2429.2 60.9 reduce-scatter.25
  2494.6 62.3 reduce-scatter.29
  2560.9 62.5 reduce-scatter.23
where the time goes:
time: 2630 us
  waiting for transfers between devices  1240 us (47%)
  other arithmetic  424 us (16%)
  local copies, waits for them, and re-layouts  381 us (14%)
  matrix products  312 us (12%)
  blocking collectives  259 us (10%)
    reduce_scatter x1, waiting for transfers between devices, body(): lax.psum_scatter(up_local, 'dp', scatter_dimension=0, tiled=True)  283 us
    reduce_scatter x1, waiting for transfers between devices, body(): lax.psum_scatter(gate_local, 'dp', scatter_dimension=0, tiled=True)  282 us
    reduce_scatter x1, waiting for transfers between devices, body(): lax.psum_scatter(down_local, 'dp', scatter_dimension=0, tiled=True)  195 us
    scatter-add x1, other arithmetic, body(): rows_grad_all = jnp.zeros((group_rows, width), jnp.float32).at[token_flat...  143 us
    scatter-add x1, other arithmetic, body(): jnp.zeros((group_rows, width), jnp.float32).at[token_flat].add(weighted)  142 us
    reduce_scatter x1, waiting for transfers between devices, body(): lax.psum_scatter(router_grad, ('dp', 'tensor'), scatter_dimension=0, tile...  133 us
    gather x2, local copies, waits for them, and re-layouts, body(): slot_weight = gates_all_f[token_of, route_of] * filled  96.5 us
    gather x2, local copies, waits for them, and re-layouts, body(): order[jnp.minimum(starts[:, None] + slots[None, :], flattened.shape[0] - 1)]  90.5 us
  transfers between devices with their start and end apart: 20, of which 11 were waited for; matrix products, arithmetic and copies ran while one was open for 34% of the time, Pallas kernels for 0%

commit v1 on v0

--- a/solution.py
+++ b/solution.py
@@ -4,7 +4,6 @@
 from jax.sharding import PartitionSpec as P
 
 HEAD_SIZE = 64
-CAP = 512
 
 
 eps_norm = 1e-06
@@ -80,34 +79,41 @@
     length_tokens = document_index.shape[1]
     my_index = lax.axis_index("tensor")
     experts = w_gate.shape[1]
-    top = routes.shape[1]
     scale = HEAD_SIZE ** (-0.5)
-    gain_one, gain_two, router_full = (
-        lax.all_gather(gain_attn, ("dp", "tensor"), axis=0, tiled=True),
-        lax.all_gather(gain_moe, ("dp", "tensor"), axis=0, tiled=True),
-        lax.all_gather(w_router, ("dp", "tensor"), axis=0, tiled=True),
-    )
-    gain_one_f = gain_one.astype(jnp.float32)
-    gain_two_f = gain_two.astype(jnp.float32)
-    full_query, full_key, full_value, full_out, full_gate, full_up, full_down = (
-        lax.all_gather(w_query, "dp", axis=0, tiled=True),
-        lax.all_gather(key_weight, "dp", axis=0, tiled=True),
-        lax.all_gather(value_weight, "dp", axis=0, tiled=True),
-        lax.all_gather(w_out, "dp", axis=0, tiled=True),
-        lax.all_gather(w_gate, "dp", axis=0, tiled=True),
-        lax.all_gather(w_up, "dp", axis=0, tiled=True),
-        lax.all_gather(w_down, "dp", axis=0, tiled=True),
-    )
+    ff_local = w_gate.shape[2]
+    small_packed = jnp.concatenate([w_router, gain_attn[:, None], gain_moe[:, None]], axis=1)
+    small_full = lax.all_gather(small_packed, ("dp", "tensor"), axis=0, tiled=True)
+    router_full = small_full[:, :experts]
+    gain_one_f = small_full[:, experts].astype(jnp.float32)
+    gain_two_f = small_full[:, experts + 1].astype(jnp.float32)
+    tokens_all = lax.all_gather(tokens, "tensor", axis=0, tiled=True)
+    attn_full = lax.all_gather(
+        jnp.concatenate([w_query, key_weight, value_weight, w_out], axis=1),
+        "dp",
+        axis=0,
+        tiled=True,
+    )
+    q_width = w_query.shape[1]
+    kv_width = key_weight.shape[1]
+    joined_width = q_width + 2 * kv_width
+    joined = attn_full[:, :joined_width]
+    full_out = attn_full[:, joined_width:]
+    full_gate, full_up, full_down = (
+        lax.all_gather(w_gate.reshape(-1, experts * ff_local), "dp", axis=0, tiled=True),
+        lax.all_gather(w_up.reshape(-1, experts * ff_local), "dp", axis=0, tiled=True),
+        lax.all_gather(w_down.reshape(-1, experts * ff_local), "dp", axis=0, tiled=True),
+    )
+    moe_grads_all = lax.all_gather(cotangent, "tensor", axis=0, tiled=True)
     tokens_f = tokens.astype(jnp.float32)
     inverse_one = lax.rsqrt(jnp.mean(tokens_f * tokens_f, axis=1, keepdims=True) + eps_norm)
-    normed_one = (tokens_f * inverse_one * gain_one_f).astype(jnp.bfloat16)
-    normed_all = lax.all_gather(normed_one, "tensor", axis=0, tiled=True)
-    q_width = full_query.shape[1]
-    kv_width = full_key.shape[1]
+    tokens_all_f = tokens_all.astype(jnp.float32)
+    inverse_all = lax.rsqrt(
+        jnp.mean(tokens_all_f * tokens_all_f, axis=1, keepdims=True) + eps_norm
+    )
+    normed_all = (tokens_all_f * inverse_all * gain_one_f).astype(jnp.bfloat16)
     heads_q = q_width // HEAD_SIZE
     heads_kv = kv_width // HEAD_SIZE
     query_group = heads_q // heads_kv
-    joined = jnp.concatenate([full_query, full_key, full_value], axis=1)
     projected = plain_dot(normed_all, joined)
     token_positions = jax.vmap(doc_positions)(document_index).reshape(-1)
     query_b = rotate_pairs(projected[:, :q_width], token_positions, heads_q, 1.0).astype(
@@ -157,87 +163,56 @@
     ).astype(jnp.float32)
     inverse_two = lax.rsqrt(jnp.mean(middle * middle, axis=1, keepdims=True) + eps_norm)
     normed_two = (middle * inverse_two * gain_two_f).astype(jnp.bfloat16)
-    logits = plain_dot(normed_two, router_full)
+    normed_two_all = lax.all_gather(normed_two, "tensor", axis=0, tiled=True)
     expert_ids = jnp.arange(experts, dtype=jnp.int32)
-    local_routes = lax.dynamic_slice_in_dim(routes, my_index * local_rows, local_rows, 0)
-    chosen = (local_routes[:, :, None] == expert_ids[None, None, :]).astype(jnp.float32)
-    picked = jnp.sum(chosen * logits[:, None, :], axis=2)
-    picked_peak = jnp.max(picked, axis=1, keepdims=True)
-    picked_exp = jnp.exp(picked - picked_peak)
-    gates_f = picked_exp / jnp.sum(picked_exp, axis=1, keepdims=True)
-    normed_two_all, gates_all = (
-        lax.all_gather(normed_two, "tensor", axis=0, tiled=True),
-        lax.all_gather(gates_f.astype(jnp.bfloat16), "tensor", axis=0, tiled=True),
-    )
-    gates_all_f = gates_all.astype(jnp.float32)
-    flattened = routes.reshape(-1)
-    order = jnp.argsort(flattened, stable=True)
-    counts = jnp.sum((flattened[:, None] == expert_ids[None, :]).astype(jnp.int32), axis=0)
-    starts = jnp.cumsum(counts) - counts
-    slots = jnp.arange(CAP, dtype=jnp.int32)
-    table = order[jnp.minimum(starts[:, None] + slots[None, :], flattened.shape[0] - 1)]
-    filled = (slots[None, :] < counts[:, None]).astype(jnp.float32)
-    token_of = table // top
-    route_of = table % top
-    token_flat = token_of.reshape(-1)
-    slot_weight = gates_all_f[token_of, route_of] * filled
-    inputs_disp = normed_two_all[token_of]
-    gate_kept = jnp.einsum(
-        "ecd,def->ecf", inputs_disp, full_gate, preferred_element_type=jnp.float32
-    )
-    up_kept = jnp.einsum("ecd,def->ecf", inputs_disp, full_up, preferred_element_type=jnp.float32)
-    active_fwd = (jax.nn.silu(gate_kept) * up_kept).astype(jnp.bfloat16)
-    result_disp = jnp.einsum(
-        "ecf,def->ecd", active_fwd, full_down, preferred_element_type=jnp.float32
-    )
-    weighted = (slot_weight[:, :, None] * result_disp).reshape(-1, width)
-    moe_all = jnp.zeros((group_rows, width), jnp.float32).at[token_flat].add(weighted)
-    moe_local = lax.psum_scatter(
-        moe_all.astype(jnp.bfloat16), "tensor", scatter_dimension=0, tiled=True
-    ).astype(jnp.float32)
-    output = (middle + moe_local).astype(jnp.bfloat16)
-    upstream = cotangent.astype(jnp.float32)
-    moe_grads_all = lax.all_gather(cotangent, "tensor", axis=0, tiled=True)
-    grads_disp = moe_grads_all[token_of]
+    member = jnp.any(routes[:, :, None] == expert_ids[None, None, :], axis=1)
+    logits_all = plain_dot(normed_two_all, router_full)
+    masked_logits = jnp.where(member, logits_all, -jnp.inf)
+    peak_logits = jnp.max(masked_logits, axis=1, keepdims=True)
+    exp_logits = jnp.exp(masked_logits - peak_logits)
+    gates_all_f = exp_logits / jnp.sum(exp_logits, axis=1, keepdims=True)
+    hidden_expert = jnp.arange(experts * ff_local, dtype=jnp.int32) // ff_local
+    spread = (expert_ids[:, None] == hidden_expert[None, :]).astype(jnp.bfloat16)
+    gates_wide = plain_dot(gates_all_f.astype(jnp.bfloat16), spread).astype(jnp.bfloat16)
+    gates_wide_f = gates_wide.astype(jnp.float32)
+    gate_kept = plain_dot(normed_two_all, full_gate)
+    up_kept = plain_dot(normed_two_all, full_up)
     sigma = jax.nn.sigmoid(gate_kept)
     swish = gate_kept * sigma
-    folded = jnp.einsum("ecd,def->ecf", grads_disp, full_down, preferred_element_type=jnp.float32)
-    gate_grad_slot = jnp.sum(active_fwd.astype(jnp.float32) * folded, axis=2) * filled
-    scaled = (slot_weight[:, :, None] * grads_disp.astype(jnp.float32)).astype(jnp.bfloat16)
-    active_grad = jnp.einsum("ecd,def->ecf", scaled, full_down, preferred_element_type=jnp.float32)
-    down_local = jnp.einsum("ecd,ecf->def", scaled, active_fwd, preferred_element_type=jnp.float32)
+    active_f = swish * up_kept
+    weighted = (active_f * gates_wide_f).astype(jnp.bfloat16)
+    down_local = dot_left_t(moe_grads_all, weighted).astype(jnp.bfloat16)
+    grad_down = lax.psum_scatter(down_local, "dp", scatter_dimension=0, tiled=True)
+    moe_all = dot_right_t(weighted, full_down).astype(jnp.bfloat16)
+    upstream = cotangent.astype(jnp.float32)
+    folded = plain_dot(moe_grads_all, full_down)
+    gates_grad_part = dot_right_t((active_f * folded).astype(jnp.bfloat16), spread)
+    active_grad = folded * gates_wide_f
     gate_pre_grad = (active_grad * up_kept * sigma * (1.0 + gate_kept * (1.0 - sigma))).astype(
         jnp.bfloat16
     )
     up_pre_grad = (active_grad * swish).astype(jnp.bfloat16)
-    gate_local = jnp.einsum(
-        "ecd,ecf->def", inputs_disp, gate_pre_grad, preferred_element_type=jnp.float32
-    )
-    up_local = jnp.einsum(
-        "ecd,ecf->def", inputs_disp, up_pre_grad, preferred_element_type=jnp.float32
-    )
-    input_grad = jnp.einsum(
-        "ecf,def->ecd", gate_pre_grad, full_gate, preferred_element_type=jnp.float32
-    ) + jnp.einsum("ecf,def->ecd", up_pre_grad, full_up, preferred_element_type=jnp.float32)
-    rows_grad_all = (
-        jnp.zeros((group_rows, width), jnp.float32)
-        .at[token_flat]
-        .add(input_grad.reshape(-1, width))
-    )
-    gates_grad_all = (
-        jnp.zeros((group_rows, top), jnp.float32).at[token_of, route_of].add(gate_grad_slot)
-    )
-    normed_two_grad, gates_grad = (
-        lax.psum_scatter(
-            rows_grad_all.astype(jnp.bfloat16), "tensor", scatter_dimension=0, tiled=True
-        ).astype(jnp.float32),
-        lax.psum_scatter(
-            gates_grad_all.astype(jnp.bfloat16), "tensor", scatter_dimension=0, tiled=True
-        ).astype(jnp.float32),
-    )
+    gate_local = dot_left_t(normed_two_all, gate_pre_grad).astype(jnp.bfloat16)
+    up_local = dot_left_t(normed_two_all, up_pre_grad).astype(jnp.bfloat16)
+    rows_grad_all = dot_right_t(gate_pre_grad, full_gate) + dot_right_t(up_pre_grad, full_up)
+    pad = jnp.zeros((group_rows, 128 - experts % 128), jnp.bfloat16)
+    expert_sums = lax.psum_scatter(
+        jnp.concatenate(
+            [rows_grad_all.astype(jnp.bfloat16), moe_all, gates_grad_part.astype(jnp.bfloat16), pad],
+            axis=1,
+        ),
+        "tensor",
+        scatter_dimension=0,
+        tiled=True,
+    ).astype(jnp.float32)
+    normed_two_grad = expert_sums[:, :width]
+    output = (middle + expert_sums[:, width : 2 * width]).astype(jnp.bfloat16)
+    gates_grad = expert_sums[:, 2 * width : 2 * width + experts]
+    gates_f = lax.dynamic_slice_in_dim(gates_all_f, my_index * local_rows, local_rows, 0)
     inner = jnp.sum(gates_f * gates_grad, axis=1, keepdims=True)
-    picked_grad = gates_f * (gates_grad - inner)
-    logits_grad = jnp.sum(chosen * picked_grad[:, :, None], axis=1).astype(jnp.bfloat16)
+    logits_grad = (gates_f * (gates_grad - inner)).astype(jnp.bfloat16)
+    grad_gate = lax.psum_scatter(gate_local, "dp", scatter_dimension=0, tiled=True)
+    grad_up = lax.psum_scatter(up_local, "dp", scatter_dimension=0, tiled=True)
     router_grad = dot_left_t(normed_two, logits_grad)
     normed_two_grad = normed_two_grad + dot_right_t(logits_grad, router_full)
     middle_part, gain_two_grad = norm_backward(middle, inverse_two, gain_two_f, normed_two_grad)
@@ -294,32 +269,33 @@
     value_pre_grad = value_grad.reshape(group_rows, kv_width).astype(jnp.bfloat16)
     joined_grad = jnp.concatenate([query_pre_grad, key_pre_grad, value_pre_grad], axis=1)
     joined_weight_grad = dot_left_t(normed_all, joined_grad)
-    piece = joined_grad
+    normed_one_part = dot_right_t(joined_grad, joined)
+    gain_one_grad = jnp.sum(normed_one_part * (tokens_all_f * inverse_all), axis=0)
     normed_one_grad = lax.psum_scatter(
-        dot_right_t(piece, joined).astype(jnp.bfloat16), "tensor", scatter_dimension=0, tiled=True
+        normed_one_part.astype(jnp.bfloat16), "tensor", scatter_dimension=0, tiled=True
     ).astype(jnp.float32)
-    tokens_part, gain_one_grad = norm_backward(tokens_f, inverse_one, gain_one_f, normed_one_grad)
+    tokens_part, _ = norm_backward(tokens_f, inverse_one, gain_one_f, normed_one_grad)
     grad_tokens = (middle_grad + tokens_part).astype(jnp.bfloat16)
-    grad_query, grad_key, grad_value, grad_out, grad_gate, grad_up, grad_down = (
-        lax.psum_scatter(joined_weight_grad[:, :q_width], "dp", scatter_dimension=0, tiled=True),
-        lax.psum_scatter(
-            joined_weight_grad[:, q_width : q_width + kv_width],
-            "dp",
-            scatter_dimension=0,
-            tiled=True,
-        ),
-        lax.psum_scatter(
-            joined_weight_grad[:, q_width + kv_width :], "dp", scatter_dimension=0, tiled=True
-        ),
-        lax.psum_scatter(out_weight_grad, "dp", scatter_dimension=0, tiled=True),
-        lax.psum_scatter(gate_local, "dp", scatter_dimension=0, tiled=True),
-        lax.psum_scatter(up_local, "dp", scatter_dimension=0, tiled=True),
-        lax.psum_scatter(down_local, "dp", scatter_dimension=0, tiled=True),
-    )
-    grad_gain_attn, grad_gain_moe, grad_router = (
-        lax.psum_scatter(gain_one_grad, ("dp", "tensor"), scatter_dimension=0, tiled=True),
-        lax.psum_scatter(gain_two_grad, ("dp", "tensor"), scatter_dimension=0, tiled=True),
-        lax.psum_scatter(router_grad, ("dp", "tensor"), scatter_dimension=0, tiled=True),
+    extra = jnp.concatenate([router_grad, gain_one_grad[:, None], gain_two_grad[:, None]], axis=1)
+    extra = jnp.pad(extra, ((0, 0), (0, 128 - (experts + 2) % 128)))
+    projections = lax.psum_scatter(
+        jnp.concatenate([joined_weight_grad, out_weight_grad, extra], axis=1).astype(jnp.bfloat16),
+        "dp",
+        scatter_dimension=0,
+        tiled=True,
+    ).astype(jnp.float32)
+    grad_query = projections[:, :q_width]
+    grad_key = projections[:, q_width : q_width + kv_width]
+    grad_value = projections[:, q_width + kv_width : joined_width]
+    grad_out = projections[:, joined_width : joined_width + q_width]
+    small = lax.psum_scatter(
+        projections[:, joined_width + q_width :], "tensor", scatter_dimension=0, tiled=True
+    )
+    grad_router = small[:, :experts]
+    grad_gain_attn = small[:, experts]
+    grad_gain_moe = small[:, experts + 1]
+    grad_gate, grad_up, grad_down = (
+        piece.astype(jnp.float32).reshape(w_gate.shape) for piece in (grad_gate, grad_up, grad_down)
     )
     return (
         output,

time: 2630 us -> 1400 us (0.53)
  other arithmetic: 424 us -> 40.7 us
  local copies, waits for them, and re-layouts: 381 us -> 47 us
  waiting for transfers between devices: 1240 us -> 1010 us
  blocking collectives: 259 us -> 44.4 us
  matrix products: 312 us -> 237 us
    reduce_scatter x11 -> x3, waiting for transfers between devices: 900 us -> 193 us  [the longest x1 149 us: body(): grad_up = lax.psum_scatter(up_local, 'dp', scatter_dimension=0, tiled=True)]
    all_gather x5 -> x6, waiting for transfers between devices: 0.03 us -> 398 us  [the longest x1 128 us: body(): lax.all_gather(w_down.reshape(-1, experts * ff_local), 'dp', axis=0, tile...]
    gather x6 -> x0, local copies, waits for them, and re-layouts: 351 us -> none  [the longest x2 96.5 us: body(): slot_weight = gates_all_f[token_of, route_of] * filled]
    scatter-add x2 -> x0, other arithmetic: 285 us -> none  [the longest x1 143 us: body(): rows_grad_all = jnp.zeros((group_rows, width), jnp.float32).at[token_flat...]
    dot_general x10 -> x0, matrix products: 251 us -> none  [the longest x1 46.6 us: body(): jnp.einsum('ecf,def->ecd', up_pre_grad, full_up, preferred_element_type=j...]
    unnamed x20 -> x19, waiting for transfers between devices: 1.5 us -> 207 us
    reduce_scatter x1, waiting for transfers between devices: 282 us -> 148 us  [body(): lax.psum_scatter(gate_local, 'dp', scatter_dimension=0, tiled=True)]
    all_gather x6 -> x1, blocking collectives: 174 us -> 44.4 us  [body(): lax.all_gather(small_packed, ('dp', 'tensor'), axis=0, tiled=True)]
  transfers between devices with their start and end apart: 20 -> 16, of which waited for: 11 -> 13; matrix products, arithmetic and copies ran while one was open for 34% -> 9% of each run, Pallas kernels for 0% -> 0%
where the time goes in v1:
time: 1400 us; the launch traced here: 1390 us
  waiting for transfers between devices  1010 us (72%)
  matrix products  237 us (17%)
  local copies, waits for them, and re-layouts  47 us (3%)
  blocking collectives  44.4 us (3%)
  other arithmetic  40.7 us (3%)
  between operations  15.4 us (1%)
    unnamed x19, waiting for transfers between devices  207 us
    reduce_scatter x1, waiting for transfers between devices, body(): grad_up = lax.psum_scatter(up_local, 'dp', scatter_dimension=0, tiled=True)  149 us
    reduce_scatter x1, waiting for transfers between devices, body(): lax.psum_scatter(gate_local, 'dp', scatter_dimension=0, tiled=True)  148 us
    all_gather x1, waiting for transfers between devices, body(): lax.all_gather(w_down.reshape(-1, experts * ff_local), 'dp', axis=0, tile...  128 us
    all_gather x1, waiting for transfers between devices, body(): lax.all_gather(w_gate.reshape(-1, experts * ff_local), 'dp', axis=0, tile...  125 us
    all_gather x1, waiting for transfers between devices, body(): lax.all_gather(w_up.reshape(-1, experts * ff_local), 'dp', axis=0, tiled=...  110 us
    dot_general x7, matrix products, plain_dot(): return jnp.dot(left, right, preferred_element_type=jnp.float32)  79.8 us
    dot_general x7, matrix products, dot_right_t(): lax.dot_general(left, right, (((1,), (1,)), ((), ())), preferred_element_...  67.7 us
  transfers between devices with their start and end apart: 16, of which 13 were waited for; matrix products, arithmetic and copies ran while one was open for 9% of the time, Pallas kernels for 0%

profile of v1, /device:TPU:0, one launch (start us, length us, event | category | flops | bytes accessed | tf_op | source)
XLA Modules:
  0.0 1393.7 jit_solution(7552265349779977638)
XLA Ops:
  11.9 44.4 %all_gather.28 = bf16[1024,34]{1,0:T(8,128)(2,1)S(1)} all-gather(bf16[32,34]{1,0:T(8,128)(2,1)S(1)} %pad_maximum_fusion.8), channel_id=1, replica_groups=mesh['dp'=8,'tensor'=4] {'dp','tensor'}, dimensions={0}, use_global_device_ids=true | all-gather | bytes 71808 | tf_op jit(solution)/shard_map/all_gather | solution.py:85
  62.7 20.3 %all-gather.11.cloned.1.call-done = bf16[1024,768]{1,0:T(8,128)(2,1)} async-done(((bf16[128,768]{1,0:T(8,128)(2,1)}), bf16[1024,768]{1,0:T(8,128)(2,1)}) %all-gather.11.cloned.1.call-update) | async-done | bytes 1572880 | tf_op jit(solution)/shard_map/all_gather | solution.py:90
  94.2 8.0 fusion.5
  102.8 7.4 fusion.19
  114.3 30.3 %reduce-scatter.15.cloned.1.call-done = bf16[256,1024]{1,0:T(8,128)(2,1)} async-done(((bf16[1024,1024]{1,0:T(8,128)(2,1)}), bf16[256,1024]{1,0:T(8,128)(2,1)}) %reduce-scatter.15.cloned.1.call-update) | async-done | bytes 524304 | tf_op jit(solution)/shard_map/reduce_scatter | solution.py:161
  156.3 15.7 %all-gather.17.cloned.1.call-done = bf16[1024,1024]{1,0:T(8,128)(2,1)} async-done(((bf16[256,1024]{1,0:T(8,128)(2,1)}), bf16[1024,1024]{1,0:T(8,128)(2,1)}) %all-gather.17.cloned.1.call-update) | async-done | bytes 2097168 | tf_op jit(solution)/shard_map/all_gather | solution.py:166
  175.1 124.6 %all-gather.21.cloned.1.call-done = bf16[1024,4096]{1,0:T(8,128)(2,1)} async-done(((bf16[128,4096]{1,0:T(8,128)(2,1)}), bf16[1024,4096]{1,0:T(8,128)(2,1)}) %all-gather.21.cloned.1.call-update) | async-done | bytes 8388624 | tf_op jit(solution)/shard_map/all_gather | solution.py:102
  299.7 16.0 %fusion.73 = f32[1024,4096]{1,0:T(8,128)} fusion(bf16[1024,1024]{1,0:T(8,128)(2,1)} %all-gather.17.cloned.1.call-done, bf16[1024,4096]{1,0:T(8,128)(2,1)} %all-gather.21.cloned.1.call-done), kind=kOutput, calls=%fused_computation.154 | convolution fusion | flops 8589934592 | bytes 27262976 | tf_op jit(solution)/shard_map/dot_general | solution.py:14
  315.7 109.9 %all-gather.19.cloned.1.call-done = bf16[1024,4096]{1,0:T(8,128)(2,1)} async-done(((bf16[128,4096]{1,0:T(8,128)(2,1)}), bf16[1024,4096]{1,0:T(8,128)(2,1)}) %all-gather.19.cloned.1.call-update) | async-done | bytes 8388624 | tf_op jit(solution)/shard_map/all_gather | solution.py:103
  425.6 14.5 %fusion.72 = f32[1024,4096]{1,0:T(8,128)} fusion(bf16[1024,1024]{1,0:T(8,128)(2,1)S(1)} %copy-done.15, bf16[1024,4096]{1,0:T(8,128)(2,1)} %all-gather.19.cloned.1.call-done), kind=kOutput, calls=%fused_computation.153 | convolution fusion | flops 8589934592 | bytes 27262976 | tf_op jit(solution)/shard_map/dot_general | solution.py:14
  440.1 8.0 all-gather.13.cloned.1.call-done
  448.1 127.9 %all-gather.15.cloned.1.call-done = bf16[1024,4096]{1,0:T(8,128)(2,1)} async-done(((bf16[128,4096]{1,0:T(8,128)(2,1)}), bf16[1024,4096]{1,0:T(8,128)(2,1)}) %all-gather.15.cloned.1.call-update) | async-done | bytes 8388624 | tf_op jit(solution)/shard_map/all_gather | solution.py:104
  575.9 16.0 %fusion.71 = f32[1024,4096]{1,0:T(8,128)} fusion(bf16[1024,1024]{1,0:T(8,128)(2,1)} %all-gather.13.cloned.1.call-done, bf16[1024,4096]{1,0:T(8,128)(2,1)} %all-gather.15.cloned.1.call-done), kind=kOutput, calls=%fused_computation.152 | convolution fusion | flops 8589934592 | bytes 27262976 | tf_op jit(solution)/shard_map/dot_general | solution.py:14
  591.9 18.0 %fusion.28 = bf16[1024,32]{0,1:T(8,128)(2,1)S(1)} fusion(f32[1024,4096]{1,0:T(8,128)} %fusion.71, f32[1024,4096]{1,0:T(8,128)} %fusion.72, s32[4096]{0:T(1024)S(1)} %add_select_fusion, f32[1024,4096]{1,0:T(8,128)} %fusion.73), kind=kOutput, calls=%fused_computation.60 | convolution fusion | flops 297959424 | bytes 50413568 | tf_op jit(solution)/shard_map/dot_general | solution.py:18
  609.9 25.3 %fusion = (bf16[1024,4096]{1,0:T(8,128)(2,1)}, bf16[1024,4096]{1,0:T(8,128)(2,1)}, bf16[1024,4096]{1,0:T(8,128)(2,1)}) fusion(f32[1024,4096]{1,0:T(8,128)} %fusion.72, f32[1024,4096]{1,0:T(8,128)} %fusion.73, f32[1024,4096]{1,0:T(8,128)} %fusion.71, s32[4096]{0:T(1024)S(1)} %add_select_fusion, f32[1024,32]{1,0:T(8,128)S(1)} %fusion.46), kind=kOutput, calls=%fused_computation.2 | convolution fusion | flops 348291072 | bytes 75644928 | tf_op jit(solution)/shard_map/dot_general | solution.py:14
  635.4 15.3 %fusion.74 = f32[1024,1024]{1,0:T(8,128)} fusion(bf16[1024,4096]{1,0:T(8,128)(2,1)} %get-tuple-element.129, bf16[1024,4096]{1,0:T(8,128)(2,1)} %all-gather.21.cloned.1.call-done), kind=kOutput, calls=%fused_computation.155 | convolution fusion | flops 8589934592 | bytes 20971520 | tf_op jit(solution)/shard_map/dot_general | solution.py:18
  650.7 15.3 %convolution_convert_fusion.3 = bf16[1024,1024]{1,0:T(8,128)(2,1)} fusion(bf16[1024,4096]{1,0:T(8,128)(2,1)} %get-tuple-element.128, bf16[1024,4096]{1,0:T(8,128)(2,1)} %all-gather.15.cloned.1.call-done), kind=kOutput, calls=%fused_computation.41 | convolution fusion | flops 8590983168 | bytes 18874368 | tf_op jit(solution)/shard_map/dot_general | solution.py:18
  666.0 11.7 add_convert_fusion
  677.8 8.1 concatenate.40
  685.9 44.4 %reduce-scatter.17.cloned.1.call-done = bf16[256,2176]{1,0:T(8,128)(2,1)} async-done(((bf16[1024,2176]{1,0:T(8,128)(2,1)}), bf16[256,2176]{1,0:T(8,128)(2,1)}) %reduce-scatter.17.cloned.1.call-update) | async-done | bytes 1114128 | tf_op jit(solution)/shard_map/reduce_scatter | solution.py:199
  736.0 22.4 %all-gather.23.cloned.1.call-done = bf16[1024,1024]{1,0:T(8,128)(2,1)} async-done(((bf16[256,1024]{1,0:T(8,128)(2,1)}), bf16[1024,1024]{1,0:T(8,128)(2,1)}) %all-gather.23.cloned.1.call-update) | async-done | bytes 2097168 | tf_op jit(solution)/shard_map/all_gather | solution.py:220
  760.9 9.3 fusion.25
  770.2 13.2 fusion.1
  783.4 8.3 fusion.3
  804.6 66.2 %reduce-scatter.25.cloned.1.call-done = bf16[128,896]{1,0:T(8,128)(2,1)} async-done(((bf16[1024,896]{1,0:T(8,128)(2,1)}), bf16[128,896]{1,0:T(8,128)(2,1)}) %reduce-scatter.25.cloned.1.call-update) | async-done | bytes 229392
  873.5 15.1 %convert_bitcast_fusion = bf16[1024,4096]{0,1:T(8,128)(2,1)} fusion(bf16[1024,4096]{1,0:T(8,128)(2,1)} %get-tuple-element.128, bf16[1024,1024]{1,0:T(8,128)(2,1)} %all-gather.13.cloned.1.call-done), kind=kOutput, calls=%fused_computation.21 | convolution fusion | flops 8594128896 | bytes 18874368 | tf_op jit(solution)/shard_map/dot_general | solution.py:24
  888.6 11.3 copy.132
  899.9 15.6 %convolution_convert_fusion.1 = bf16[1024,4096]{1,0:T(8,128)(2,1)} fusion(bf16[1024,1024]{1,0:T(8,128)(2,1)} %all-gather.17.cloned.1.call-done, bf16[1024,4096]{1,0:T(8,128)(2,1)} %get-tuple-element.129), kind=kOutput, calls=%fused_computation.25 | convolution fusion | flops 8594128896 | bytes 18874368 | tf_op jit(solution)/shard_map/dot_general | solution.py:24
  915.6 15.2 %convolution_convert_fusion = bf16[1024,4096]{1,0:T(8,128)(2,1)} fusion(bf16[1024,1024]{1,0:T(8,128)(2,1)} %all-gather.17.cloned.1.call-done, bf16[1024,4096]{1,0:T(8,128)(2,1)} %get-tuple-element.130), kind=kOutput, calls=%fused_computation.24 | convolution fusion | flops 8594128896 | bytes 18874368 | tf_op jit(solution)/shard_map/dot_general | solution.py:24
  941.2 138.9 %reduce-scatter.29.cloned.1.call-done = bf16[128,4096]{1,0:T(8,128)(2,1)} async-done(((bf16[1024,4096]{1,0:T(8,128)(2,1)}), bf16[128,4096]{1,0:T(8,128)(2,1)}) %reduce-scatter.29.cloned.1.call-update) | async-done | bytes 1048592
  1083.5 148.2 %reduce-scatter.21.cloned.1.call-done = bf16[128,4096]{1,0:T(8,128)(2,1)} async-done(((bf16[1024,4096]{1,0:T(8,128)(2,1)}), bf16[128,4096]{1,0:T(8,128)(2,1)}) %reduce-scatter.21.cloned.1.call-update) | async-done | bytes 1048592 | tf_op jit(solution)/shard_map/reduce_scatter | solution.py:214
  1234.7 148.9 %reduce-scatter.23.cloned.1.call-done = bf16[128,4096]{1,0:T(8,128)(2,1)} async-done(((bf16[1024,4096]{1,0:T(8,128)(2,1)}), bf16[128,4096]{1,0:T(8,128)(2,1)}) %reduce-scatter.23.cloned.1.call-update) | async-done | bytes 1048592 | tf_op jit(solution)/shard_map/reduce_scatter | solution.py:215
  (227 shorter events, 84.8 us)
Async XLA Ops:
  7.2 53.5 %all-gather.9.cloned.1.call-start = ((), (), s32[]{:S(2)}) async-start(), calls=%async_computation.8 | async-start | bytes 2621440 | tf_op jit(solution)/shard_map/all_gather | solution.py:89
  7.9 75.1 %all-gather.11.cloned.1.call-start = ((), (), s32[]{:S(2)}) async-start(), calls=%async_computation.9 | async-start | bytes 1769472 | tf_op jit(solution)/shard_map/all_gather | solution.py:90
  9.6 135.1 %reduce-scatter.15.cloned.1.call-start = ((), (), s32[]{:S(2)}) async-start(), calls=%async_computation.10 | async-start | bytes 2621440 | tf_op jit(solution)/shard_map/reduce_scatter | solution.py:161
  56.3 115.7 %copy-start.6 = (bf16[1024,34]{1,0:T(8,128)(2,1)}, bf16[1024,34]{1,0:T(8,128)(2,1)S(1)}, u32[]{:S(2)}) copy-start(bf16[1024,34]{1,0:T(8,128)(2,1)S(1)} %all_gather.28) | copy-start | bytes 208900
  56.7 89.9 %copy-start.29 = (f32[1024]{0:T(1024)}, f32[1024]{0:T(1024)S(1)}, u32[]{:S(2)}) copy-start(f32[1024]{0:T(1024)S(1)} %get-tuple-element.126) | copy-start | bytes 12292
  102.8 41.9 %copy-start = (bf16[256,1024]{1,0:T(8,128)(2,1)S(1)}, bf16[256,1024]{1,0:T(8,128)(2,1)}, u32[]{:S(2)}) copy-start(bf16[256,1024]{1,0:T(8,128)(2,1)} %param.14) | copy-start | bytes 1572868
  110.3 40.6 %copy-start.20 = (bf16[128,32,128]{2,1,0:T(8,128)(2,1)S(1)}, bf16[128,32,128]{2,1,0:T(8,128)(2,1)}, u32[]{:S(2)}) copy-start(bf16[128,32,128]{2,1,0:T(8,128)(2,1)} %param.26) | copy-start | bytes 3145732
  114.3 41.6 %copy-start.37 = (s32[1024,8]{0,1:T(8,128)S(1)}, s32[1024,8]{0,1:T(8,128)}, u32[]{:S(2)}) copy-start(s32[1024,8]{0,1:T(8,128)} %param.17) | copy-start | bytes 98308
  114.3 57.7 %all-gather.17.cloned.1.call-start = ((), (), s32[]{:S(2)}) async-start(), calls=%async_computation.13 | async-start | bytes 2621440 | tf_op jit(solution)/shard_map/all_gather | solution.py:166
  149.2 150.5 %all-gather.21.cloned.1.call-start = ((), (), s32[]{:S(2)}) async-start(), calls=%async_computation.15 | async-start | bytes 9437184 | tf_op jit(solution)/shard_map/all_gather | solution.py:102
  150.9 274.7 %all-gather.19.cloned.1.call-start = ((), (), s32[]{:S(2)}) async-start(), calls=%async_computation.14 | async-start | bytes 9437184 | tf_op jit(solution)/shard_map/all_gather | solution.py:103
  152.4 295.7 %all-gather.13.cloned.1.call-start = ((), (), s32[]{:S(2)}) async-start(), calls=%async_computation.11 | async-start | bytes 2621440 | tf_op jit(solution)/shard_map/all_gather | solution.py:106
  153.1 422.8 %all-gather.15.cloned.1.call-start = ((), (), s32[]{:S(2)}) async-start(), calls=%async_computation.12 | async-start | bytes 9437184 | tf_op jit(solution)/shard_map/all_gather | solution.py:104
  155.8 574.5 %reduce-scatter.17.cloned.1.call-start = ((), (), s32[]{:S(2)}) async-start(), calls=%async_computation.16 | async-start | bytes 5570560 | tf_op jit(solution)/shard_map/reduce_scatter | solution.py:199
  175.1 250.5 %copy-start.15 = (bf16[1024,1024]{1,0:T(8,128)(2,1)S(1)}, bf16[1024,1024]{1,0:T(8,128)(2,1)}, u32[]{:S(2)}) copy-start(bf16[1024,1024]{1,0:T(8,128)(2,1)} %all-gather.17.cloned.1.call-done) | copy-start | bytes 6291460
  677.7 55.4 %copy-start.1 = (bf16[256,1024]{1,0:T(8,128)(2,1)S(1)}, bf16[256,1024]{1,0:T(8,128)(2,1)}, u32[]{:S(2)}) copy-start(bf16[256,1024]{1,0:T(8,128)(2,1)} %param.14) | copy-start | bytes 1572868
  677.7 55.4 %copy-start.2 = (bf16[256,1024]{1,0:T(8,128)(2,1)S(1)}, bf16[256,1024]{1,0:T(8,128)(2,1)}, u32[]{:S(2)}) copy-start(bf16[256,1024]{1,0:T(8,128)(2,1)} %reduce-scatter.15.cloned.1.call-done) | copy-start | bytes 1572868
  677.7 55.4 %copy-start.7 = (bf16[1024,34]{1,0:T(8,128)(2,1)S(1)}, bf16[1024,34]{1,0:T(8,128)(2,1)}, u32[]{:S(2)}) copy-start(bf16[1024,34]{1,0:T(8,128)(2,1)} %copy-done.6) | copy-start | bytes 208900
  677.7 55.4 %copy-start.30 = (f32[1024]{0:T(1024)S(1)}, f32[1024]{0:T(1024)}, u32[]{:S(2)}) copy-start(f32[1024]{0:T(1024)} %copy-done.29) | copy-start | bytes 12292
  677.7 55.4 %copy-start.39 = (f32[256]{0:T(256)S(1)}, f32[256]{0:T(256)}, u32[]{:S(2)}) copy-start(f32[256]{0:T(256)} %copy-done.38) | copy-start | bytes 3076
  677.7 56.6 %copy-start.5 = (bf16[256,1024]{1,0:T(8,128)(2,1)S(1)}, bf16[256,1024]{1,0:T(8,128)(2,1)}, u32[]{:S(2)}) copy-start(bf16[256,1024]{1,0:T(8,128)(2,1)} %param.15) | copy-start | bytes 1572868
  677.7 56.6 %copy-start.40 = (f32[256]{0:T(256)S(1)}, f32[256]{0:T(256)}, u32[]{:S(2)}) copy-start(f32[256]{0:T(256)} %get-tuple-element.155) | copy-start | bytes 3076
  685.8 49.9 %copy-start.32 = (f32[2,2,1024]{2,1,0:T(2,128)S(1)}, f32[2,2,1024]{2,1,0:T(2,128)}, u32[]{:S(2)}) copy-start(f32[2,2,1024]{2,1,0:T(2,128)} %copy-done.31) | copy-start | bytes 49156
  685.8 49.9 %copy-start.34 = (f32[2,2,1024]{2,1,0:T(2,128)S(1)}, f32[2,2,1024]{2,1,0:T(2,128)}, u32[]{:S(2)}) copy-start(f32[2,2,1024]{2,1,0:T(2,128)} %copy-done.33) | copy-start | bytes 49156
  685.8 49.9 %copy-start.4 = (bf16[256,1024]{1,0:T(8,128)(2,1)S(1)}, bf16[256,1024]{1,0:T(8,128)(2,1)}, u32[]{:S(2)}) copy-start(bf16[256,1024]{1,0:T(8,128)(2,1)} %multiply_convert_fusion.6) | copy-start | bytes 1572868
  685.8 72.5 %all-gather.23.cloned.1.call-start = ((), (), s32[]{:S(2)}) async-start(), calls=%async_computation.17 | async-start | bytes 2621440 | tf_op jit(solution)/shard_map/all_gather | solution.py:220
  735.6 135.2 %reduce-scatter.25.cloned.1.call-start = ((), (), s32[]{:S(2)}) async-start(), calls=%async_computation.21 | async-start | bytes 2064384
  804.5 130.0 %reduce-scatter.27.cloned.1.call-start = ((), (), s32[]{:S(2)}) async-start(), calls=%async_computation.22 | async-start | bytes 81920
  872.7 63.9 %reduce-scatter.19.cloned.1.call-start = ((), (), s32[]{:S(2)}) async-start(), calls=%async_computation.18 | async-start | bytes 2621440 | tf_op jit(solution)/shard_map/reduce_scatter | solution.py:274
  873.4 206.7 %reduce-scatter.29.cloned.1.call-start = ((), (), s32[]{:S(2)}) async-start(), calls=%async_computation.23 | async-start | bytes 9437184
  899.9 331.7 %reduce-scatter.21.cloned.1.call-start = ((), (), s32[]{:S(2)}) async-start(), calls=%async_computation.19 | async-start | bytes 9437184 | tf_op jit(solution)/shard_map/reduce_scatter | solution.py:214
  915.6 468.1 %reduce-scatter.23.cloned.1.call-start = ((), (), s32[]{:S(2)}) async-start(), calls=%async_computation.20 | async-start | bytes 9437184 | tf_op jit(solution)/shard_map/reduce_scatter | solution.py:215
  (39 other events, 436.2 us)
Sparse Core Ops, SparseCore 0:
  9.6 26.2 all-gather.8
  38.6 44.3 all-gather.10
  114.4 30.2 reduce-scatter.14
  149.3 22.5 all-gather.16
  174.7 124.9 all-gather.20
  302.5 123.1 all-gather.18
  427.2 20.7 all-gather.12
  451.0 124.9 all-gather.14
  686.0 44.3 reduce-scatter.16
  735.7 22.5 all-gather.22
  804.6 66.1 reduce-scatter.24
  874.3 18.2 reduce-scatter.26
  895.7 31.4 reduce-scatter.18
  931.1 148.9 reduce-scatter.28
  1083.6 148.0 reduce-scatter.20
  1235.6 148.0 reduce-scatter.22

commit v2 on v1

--- a/solution.py
+++ b/solution.py
@@ -53,6 +53,78 @@
     gain_grad = jnp.sum(upstream * field * inverse, axis=0)
     inner = jnp.mean(scaled * field, axis=1, keepdims=True)
     return (inverse * scaled - field * inverse**3 * inner, gain_grad)
+
+
+def ring_of(size):
+    if size % 2:
+        return list(range(size))
+    return list(range(0, size, 2)) + list(range(size - 1, 0, -2))
+
+
+def ring_moves(ring, turn):
+    size = len(ring)
+    return [(ring[i], ring[(i + turn) % size]) for i in range(size)]
+
+
+def ring_owner(ring, turn, back):
+    size = len(ring)
+    table = [0] * size
+    for place in range(size):
+        table[ring[place]] = ring[(place - turn * back) % size]
+    return jnp.asarray(table, jnp.int32)[lax.axis_index("dp")]
+
+
+class RingGather:
+    def __init__(self, first, second, ring):
+        self.ring, self.step, self.rows = ring, 0, first.shape[0]
+        self.held = [first, second]
+        self.full = [
+            jnp.zeros((len(ring) * self.rows, piece.shape[1]), piece.dtype) for piece in self.held
+        ]
+        self.place()
+
+    def place(self):
+        for which, turn in ((0, 1), (1, -1)):
+            owner = ring_owner(self.ring, turn, self.step)
+            self.full[which] = lax.dynamic_update_slice_in_dim(
+                self.full[which], self.held[which], owner * self.rows, 0
+            )
+
+    def advance(self, steps, field=None):
+        for _ in range(min(steps, len(self.ring) - 1 - self.step)):
+            self.step += 1
+            self.held = [
+                lax.ppermute(self.held[which], "dp", ring_moves(self.ring, turn))
+                for which, turn in ((0, 1), (1, -1))
+            ]
+            self.place()
+        if field is not None:
+            field, self.held = lax.optimization_barrier((field, self.held))
+        return field
+
+
+class RingScatter:
+    def __init__(self, first, second, ring):
+        self.ring, self.step = ring, 0
+        self.rows = first.shape[0] // len(ring)
+        self.fields = (first, second)
+        self.sums = [self.term(0, 1), self.term(1, -1)]
+
+    def term(self, which, turn):
+        owner = ring_owner(self.ring, turn, self.step + 1)
+        return lax.dynamic_slice_in_dim(self.fields[which], owner * self.rows, self.rows, 0)
+
+    def advance(self, steps, field=None):
+        last = len(self.ring) - 1
+        for _ in range(min(steps, last - self.step)):
+            self.step += 1
+            for which, turn in ((0, 1), (1, -1)):
+                came = lax.ppermute(self.sums[which], "dp", ring_moves(self.ring, turn))
+                total = came.astype(jnp.float32) + self.term(which, turn).astype(jnp.float32)
+                self.sums[which] = total if self.step == last else total.astype(jnp.bfloat16)
+        if field is not None:
+            field, self.sums = lax.optimization_barrier((field, self.sums))
+        return field
 
 
 def body(
@@ -96,13 +168,20 @@
     q_width = w_query.shape[1]
     kv_width = key_weight.shape[1]
     joined_width = q_width + 2 * kv_width
+    dp_size = lax.axis_size("dp")
+    ring = ring_of(dp_size) if 2 < dp_size <= 16 else None
+    flat_gate = w_gate.reshape(-1, experts * ff_local)
+    flat_up = w_up.reshape(-1, experts * ff_local)
+    flat_down = w_down.reshape(-1, experts * ff_local)
+    full_gate = lax.all_gather(flat_gate, "dp", axis=0, tiled=True)
+    if ring is None:
+        full_up = lax.all_gather(flat_up, "dp", axis=0, tiled=True)
+        full_down = lax.all_gather(flat_down, "dp", axis=0, tiled=True)
+    else:
+        gathering = RingGather(flat_up, flat_down, ring)
+        attn_full = gathering.advance(2, attn_full)
     joined = attn_full[:, :joined_width]
     full_out = attn_full[:, joined_width:]
-    full_gate, full_up, full_down = (
-        lax.all_gather(w_gate.reshape(-1, experts * ff_local), "dp", axis=0, tiled=True),
-        lax.all_gather(w_up.reshape(-1, experts * ff_local), "dp", axis=0, tiled=True),
-        lax.all_gather(w_down.reshape(-1, experts * ff_local), "dp", axis=0, tiled=True),
-    )
     moe_grads_all = lax.all_gather(cotangent, "tensor", axis=0, tiled=True)
     tokens_f = tokens.astype(jnp.float32)
     inverse_one = lax.rsqrt(jnp.mean(tokens_f * tokens_f, axis=1, keepdims=True) + eps_norm)
@@ -158,12 +237,20 @@
     )
     attended_all = attended_rows.reshape(group_rows, q_width)
     piece = attended_all
-    middle = tokens_f + lax.psum_scatter(
-        dot_right_t(piece, full_out).astype(jnp.bfloat16), "tensor", scatter_dimension=0, tiled=True
-    ).astype(jnp.float32)
+    branch = dot_right_t(piece, full_out).astype(jnp.bfloat16)
+    if ring is not None:
+        branch = gathering.advance(3, branch)
+        branch, full_gate = lax.optimization_barrier((branch, full_gate))
+    branch = lax.psum_scatter(branch, "tensor", scatter_dimension=0, tiled=True)
+    if ring is not None:
+        branch = gathering.advance(1, branch)
+    middle = tokens_f + branch.astype(jnp.float32)
     inverse_two = lax.rsqrt(jnp.mean(middle * middle, axis=1, keepdims=True) + eps_norm)
     normed_two = (middle * inverse_two * gain_two_f).astype(jnp.bfloat16)
     normed_two_all = lax.all_gather(normed_two, "tensor", axis=0, tiled=True)
+    if ring is not None:
+        gathering.advance(dp_size)
+        full_up, full_down = gathering.full
     expert_ids = jnp.arange(experts, dtype=jnp.int32)
     member = jnp.any(routes[:, :, None] == expert_ids[None, None, :], axis=1)
     logits_all = plain_dot(normed_two_all, router_full)
@@ -196,23 +283,30 @@
     up_local = dot_left_t(normed_two_all, up_pre_grad).astype(jnp.bfloat16)
     rows_grad_all = dot_right_t(gate_pre_grad, full_gate) + dot_right_t(up_pre_grad, full_up)
     pad = jnp.zeros((group_rows, 128 - experts % 128), jnp.bfloat16)
-    expert_sums = lax.psum_scatter(
-        jnp.concatenate(
-            [rows_grad_all.astype(jnp.bfloat16), moe_all, gates_grad_part.astype(jnp.bfloat16), pad],
-            axis=1,
-        ),
-        "tensor",
-        scatter_dimension=0,
-        tiled=True,
-    ).astype(jnp.float32)
+    to_sum = jnp.concatenate(
+        [rows_grad_all.astype(jnp.bfloat16), moe_all, gates_grad_part.astype(jnp.bfloat16), pad],
+        axis=1,
+    )
+    if ring is not None:
+        scattering = RingScatter(gate_local, up_local, ring)
+        to_sum = scattering.advance(1, to_sum)
+        to_sum, grad_down = lax.optimization_barrier((to_sum, grad_down))
+    expert_sums = lax.psum_scatter(to_sum, "tensor", scatter_dimension=0, tiled=True)
+    if ring is not None:
+        expert_sums = scattering.advance(3, expert_sums)
+    expert_sums = expert_sums.astype(jnp.float32)
     normed_two_grad = expert_sums[:, :width]
     output = (middle + expert_sums[:, width : 2 * width]).astype(jnp.bfloat16)
     gates_grad = expert_sums[:, 2 * width : 2 * width + experts]
     gates_f = lax.dynamic_slice_in_dim(gates_all_f, my_index * local_rows, local_rows, 0)
     inner = jnp.sum(gates_f * gates_grad, axis=1, keepdims=True)
     logits_grad = (gates_f * (gates_grad - inner)).astype(jnp.bfloat16)
-    grad_gate = lax.psum_scatter(gate_local, "dp", scatter_dimension=0, tiled=True)
-    grad_up = lax.psum_scatter(up_local, "dp", scatter_dimension=0, tiled=True)
+    if ring is None:
+        grad_gate = lax.psum_scatter(gate_local, "dp", scatter_dimension=0, tiled=True)
+        grad_up = lax.psum_scatter(up_local, "dp", scatter_dimension=0, tiled=True)
+    else:
+        scattering.advance(dp_size)
+        grad_gate, grad_up = scattering.sums
     router_grad = dot_left_t(normed_two, logits_grad)
     normed_two_grad = normed_two_grad + dot_right_t(logits_grad, router_full)
     middle_part, gain_two_grad = norm_backward(middle, inverse_two, gain_two_f, normed_two_grad)

time: 1400 us -> 973 us (0.69)
  waiting for transfers between devices: 1010 us -> 422 us
  starting transfers between devices: 0.83 us -> 53.7 us
  local copies, waits for them, and re-layouts: 47 us -> 96.4 us
  blocking collectives: 44.4 us -> 72.7 us
  other arithmetic: 40.7 us -> 67.3 us
    reduce_scatter x4 -> x2, waiting for transfers between devices: 372 us -> 0.01 us  [the longest x1 0.01 us: body(): branch = lax.psum_scatter(branch, 'tensor', scatter_dimension=0, tiled=True)]
    all_gather x3 -> x1, waiting for transfers between devices: 362 us -> 0.01 us  [body(): full_gate = lax.all_gather(flat_gate, 'dp', axis=0, tiled=True)]
    ppermute x0 -> x28, waiting for transfers between devices: none -> 261 us  [the longest x14 161 us: advance(): lax.ppermute(self.held[which], 'dp', ring_moves(self.ring, turn))]
    unnamed x19 -> x15, waiting for transfers between devices: 207 us -> 139 us
    ppermute x0 -> x28, starting transfers between devices: none -> 52.6 us  [the longest x14 38.7 us: advance(): lax.ppermute(self.held[which], 'dp', ring_moves(self.ring, turn))]
    dynamic_update_slice x0 -> x16, local copies, waits for them, and re-layouts: none -> 30.4 us  [place(): lax.dynamic_update_slice_in_dim(self.full[which], self.held[which], owner...]
    all_gather x1, blocking collectives: 44.4 us -> 72.7 us  [body(): lax.all_gather(small_packed, ('dp', 'tensor'), axis=0, tiled=True)]
    convert_element_type x1 -> x13, other arithmetic: 1.39 us -> 28.5 us  [the longest x12 27.1 us: advance(): total.astype(jnp.bfloat16)]
  transfers between devices with their start and end apart: 16 -> 40, of which waited for: 13 -> 19; matrix products, arithmetic and copies ran while one was open for 9% -> 25% of each run, Pallas kernels for 0% -> 0%
where the time goes in v2:
time: 973 us; the launch traced here: 963 us
  waiting for transfers between devices  422 us (43%)
  matrix products  231 us (24%)
  local copies, waits for them, and re-layouts  96.4 us (10%)
  blocking collectives  72.7 us (7%)
  other arithmetic  67.3 us (7%)
  starting transfers between devices  53.7 us (6%)
  between operations  20.5 us (2%)
    ppermute x14, waiting for transfers between devices, advance(): lax.ppermute(self.held[which], 'dp', ring_moves(self.ring, turn))  161 us
    unnamed x15, waiting for transfers between devices  139 us
    ppermute x14, waiting for transfers between devices, advance(): came = lax.ppermute(self.sums[which], 'dp', ring_moves(self.ring, turn))  99.2 us
    dot_general x7, matrix products, plain_dot(): return jnp.dot(left, right, preferred_element_type=jnp.float32)  80.8 us
    all_gather x1, blocking collectives, body(): lax.all_gather(small_packed, ('dp', 'tensor'), axis=0, tiled=True)  72.7 us
    dot_general x7, matrix products, dot_right_t(): lax.dot_general(left, right, (((1,), (1,)), ((), ())), preferred_element_...  68.8 us
    dot_general x6, matrix products, dot_left_t(): lax.dot_general(left, right, (((0,), (0,)), ((), ())), preferred_element_...  39.5 us
    unnamed x160, local copies, waits for them, and re-layouts  39.4 us
  transfers between devices with their start and end apart: 40, of which 19 were waited for; matrix products, arithmetic and copies ran while one was open for 25% of the time, Pallas kernels for 0%

profile of v2, /device:TPU:0, one launch (start us, length us, event | category | flops | bytes accessed | tf_op | source)
XLA Modules:
  0.0 963.0 jit_solution(5750000404543273308)
XLA Ops:
  21.0 72.7 %all_gather.22 = bf16[1024,34]{1,0:T(8,128)(2,1)S(1)} all-gather(bf16[32,34]{1,0:T(8,128)(2,1)S(1)} %pad_maximum_fusion.8), channel_id=1, replica_groups=mesh['dp'=8,'tensor'=4] {'dp','tensor'}, dimensions={0}, use_global_device_ids=true | all-gather | bytes 71808 | tf_op jit(solution)/shard_map/all_gather | solution.py:157
  99.6 51.8 %collective-permute-done.3 = bf16[128,4096]{1,0:T(8,128)(2,1)S(1)} collective-permute-done((bf16[128,4096]{1,0:T(8,128)(2,1)S(1)}, bf16[128,4096]{1,0:T(8,128)(2,1)S(1)}, u32[]{:S(2)}, u32[]{:S(2)}) %collective-permute-start.3) | collective-permute-done | bytes 1048608 | tf_op jit(solution)/shard_map/ppermute | solution.py:97
  160.3 31.3 %collective-permute-done.4 = bf16[128,4096]{1,0:T(8,128)(2,1)} collective-permute-done((bf16[128,4096]{1,0:T(8,128)(2,1)}, bf16[128,4096]{1,0:T(8,128)(2,1)}, u32[]{:S(2)}, u32[]{:S(2)}) %collective-permute-start.4) | collective-permute-done | bytes 1048608 | tf_op jit(solution)/shard_map/ppermute | solution.py:97
  211.9 8.1 fusion.6
  220.0 22.9 %collective-permute-done.5 = bf16[128,4096]{1,0:T(8,128)(2,1)} collective-permute-done((bf16[128,4096]{1,0:T(8,128)(2,1)}, bf16[128,4096]{1,0:T(8,128)(2,1)}, u32[]{:S(2)}, u32[]{:S(2)}) %collective-permute-start.5) | collective-permute-done | bytes 1048608 | tf_op jit(solution)/shard_map/ppermute | solution.py:97
  242.9 19.6 %collective-permute-start.6 = (bf16[128,4096]{1,0:T(8,128)(2,1)}, bf16[128,4096]{1,0:T(8,128)(2,1)}, u32[]{:S(2)}, u32[]{:S(2)}) collective-permute-start(bf16[128,4096]{1,0:T(8,128)(2,1)} %collective-permute-done.5), channel_id=1, source_target_pairs={{0,8},{8,16},{16,24},{24,28},{28,20},{20,12},{12,4},{4,0},{1,9},{9... | collective-permute-start | bytes 3145736 | tf_op jit(solution)/shard_map/ppermute | solution.py:97
  277.8 11.8 %collective-permute-done.6 = bf16[128,4096]{1,0:T(8,128)(2,1)} collective-permute-done((bf16[128,4096]{1,0:T(8,128)(2,1)}, bf16[128,4096]{1,0:T(8,128)(2,1)}, u32[]{:S(2)}, u32[]{:S(2)}) %collective-permute-start.6) | collective-permute-done | bytes 1048608 | tf_op jit(solution)/shard_map/ppermute | solution.py:97
  334.8 14.9 %collective-permute-done.10 = bf16[128,4096]{1,0:T(8,128)(2,1)S(1)} collective-permute-done((bf16[128,4096]{1,0:T(8,128)(2,1)}, bf16[128,4096]{1,0:T(8,128)(2,1)S(1)}, u32[]{:S(2)}, u32[]{:S(2)}) %collective-permute-start.10) | collective-permute-done | bytes 1048608 | tf_op jit(solution)/shard_map/ppermute | solution.py:97
  362.3 15.7 %collective-permute-done.12 = bf16[128,4096]{1,0:T(8,128)(2,1)} collective-permute-done((bf16[128,4096]{1,0:T(8,128)(2,1)S(1)}, bf16[128,4096]{1,0:T(8,128)(2,1)}, u32[]{:S(2)}, u32[]{:S(2)}) %collective-permute-start.12) | collective-permute-done | bytes 1048608 | tf_op jit(solution)/shard_map/ppermute | solution.py:97
  382.6 16.2 %fusion.75 = f32[4096,1024]{1,0:T(8,128)} fusion(bf16[1024,4096]{1,0:T(8,128)(2,1)} %constant_dynamic-update-slice_fusion.8, bf16[1024,1024]{1,0:T(8,128)(2,1)} %all-gather.13.cloned.1.call-done), kind=kOutput, calls=%fused_computation.183 | convolution fusion | flops 8589934592 | bytes 27262976 | tf_op jit(solution)/shard_map/dot_general | solution.py:14
  401.9 16.3 %fusion.76 = f32[1024,4096]{0,1:T(8,128)} fusion(bf16[1024,1024]{1,0:T(8,128)(2,1)} %all-gather.15.cloned.1.call-done, bf16[1024,4096]{1,0:T(8,128)(2,1)} %constant_dynamic-update-slice_fusion), kind=kOutput, calls=%fused_computation.184 | convolution fusion | flops 8589934592 | bytes 27262976 | tf_op jit(solution)/shard_map/dot_general | solution.py:14
  418.3 14.7 %fusion.77 = f32[1024,4096]{0,1:T(8,128)} fusion(bf16[1024,1024]{1,0:T(8,128)(2,1)S(1)} %copy-done.20, bf16[1024,4096]{1,0:T(8,128)(2,1)} %all-gather.11.cloned.1.call-done), kind=kOutput, calls=%fused_computation.185 | convolution fusion | flops 8589934592 | bytes 27262976 | tf_op jit(solution)/shard_map/dot_general | solution.py:14
  433.0 25.4 %fusion = (bf16[1024,4096]{0,1:T(8,128)(2,1)}, bf16[1024,4096]{0,1:T(8,128)(2,1)}, bf16[1024,4096]{0,1:T(8,128)(2,1)}) fusion(f32[1024,4096]{0,1:T(8,128)} %fusion.76, f32[1024,4096]{0,1:T(8,128)} %fusion.77, f32[4096,1024]{1,0:T(8,128)} %fusion.75, s32[4096]{0:T(1024)S(1)} %add_select_fusion, f32[1024,32]{1,0:T(8,128)S(1)} %fusion.50), kind=kOutput, calls=%fused_computation.2 | convolution fusion | flops 348291072 | bytes 75644928 | tf_op jit(solution)/shard_map/dot_general | solution.py:14
  458.4 14.6 %convert_bitcast_fusion = bf16[1024,4096]{0,1:T(8,128)(2,1)} fusion(bf16[1024,4096]{0,1:T(8,128)(2,1)} %get-tuple-element.166, bf16[1024,1024]{1,0:T(8,128)(2,1)S(1)} %copy-done.59), kind=kOutput, calls=%fused_computation.23 | convolution fusion | flops 8594128896 | bytes 18874368 | tf_op jit(solution)/shard_map/dot_general | solution.py:24
  473.0 12.0 %copy.193 = bf16[1024,4096]{1,0:T(8,128)(2,1)} copy(bf16[1024,4096]{0,1:T(8,128)(2,1)} %convert_bitcast_fusion) | data formatting | bytes 16777216
  485.3 11.3 %convolution_convert_fusion.1 = bf16[1024,4096]{1,0:T(8,128)(2,1)S(1)} fusion(bf16[1024,1024]{1,0:T(8,128)(2,1)S(1)} %copy-done.20, bf16[1024,4096]{0,1:T(8,128)(2,1)} %get-tuple-element.167), kind=kOutput, calls=%fused_computation.26 | convolution fusion | flops 8594128896 | bytes 18874368 | tf_op jit(solution)/shard_map/dot_general | solution.py:24
  500.3 11.3 %convolution_convert_fusion = bf16[1024,4096]{1,0:T(8,128)(2,1)S(1)} fusion(bf16[1024,1024]{1,0:T(8,128)(2,1)S(1)} %copy-done.20, bf16[1024,4096]{0,1:T(8,128)(2,1)} %get-tuple-element.168), kind=kOutput, calls=%fused_computation.25 | convolution fusion | flops 8594128896 | bytes 18874368 | tf_op jit(solution)/shard_map/dot_general | solution.py:24
  513.6 14.1 %fusion.78 = f32[1024,1024]{1,0:T(8,128)S(1)} fusion(bf16[1024,4096]{0,1:T(8,128)(2,1)} %get-tuple-element.167, bf16[1024,4096]{1,0:T(8,128)(2,1)} %all-gather.11.cloned.1.call-done), kind=kOutput, calls=%fused_computation.186 | convolution fusion | flops 8589934592 | bytes 20971520 | tf_op jit(solution)/shard_map/dot_general | solution.py:18
  527.7 13.9 %add_convert_fusion = bf16[1024,1024]{1,0:T(8,128)(2,1)S(1)} fusion(f32[1024,1024]{1,0:T(8,128)S(1)} %fusion.78, bf16[1024,4096]{0,1:T(8,128)(2,1)} %get-tuple-element.168, bf16[1024,4096]{1,0:T(8,128)(2,1)} %constant_dynamic-update-slice_fusion), kind=kOutput, calls=%fused_computation.36 | convolution fusion | flops 8592031744 | bytes 23068672 | tf_op jit(solution)/shard_map/dot_general | solution.py:18
  541.6 18.4 %fusion.30 = bf16[1024,32]{0,1:T(8,128)(2,1)S(1)} fusion(f32[4096,1024]{1,0:T(8,128)} %fusion.75, f32[1024,4096]{0,1:T(8,128)} %fusion.76, s32[4096]{0:T(1024)S(1)} %add_select_fusion, f32[1024,4096]{0,1:T(8,128)} %fusion.77), kind=kOutput, calls=%fused_computation.73 | convolution fusion | flops 297959424 | bytes 50413568 | tf_op jit(solution)/shard_map/dot_general | solution.py:18
  560.0 15.1 %convolution_convert_fusion.3 = bf16[1024,1024]{1,0:T(8,128)(2,1)} fusion(bf16[1024,4096]{0,1:T(8,128)(2,1)} %get-tuple-element.166, bf16[1024,4096]{1,0:T(8,128)(2,1)} %constant_dynamic-update-slice_fusion.8), kind=kOutput, calls=%fused_computation.54 | convolution fusion | flops 8590983168 | bytes 18874368 | tf_op jit(solution)/shard_map/dot_general | solution.py:18
  586.4 65.8 %reduce-scatter.19.cloned.1.call-done = bf16[128,4096]{1,0:T(8,128)(2,1)} async-done(((bf16[1024,4096]{1,0:T(8,128)(2,1)}), bf16[128,4096]{1,0:T(8,128)(2,1)}) %reduce-scatter.19.cloned.1.call-update) | async-done | bytes 1048592
  656.7 23.0 %collective-permute-done.16 = bf16[128,4096]{1,0:T(8,128)(2,1)S(1)} collective-permute-done((bf16[128,4096]{1,0:T(8,128)(2,1)S(1)}, bf16[128,4096]{1,0:T(8,128)(2,1)S(1)}, u32[]{:S(2)}, u32[]{:S(2)}) %collective-permute-start.16) | collective-permute-done | bytes 1048608 | tf_op jit(solution)/shard_map/ppermute | solution.py:122
  684.8 20.6 %collective-permute-done.17 = bf16[128,4096]{1,0:T(8,128)(2,1)S(1)} collective-permute-done((bf16[128,4096]{1,0:T(8,128)(2,1)S(1)}, bf16[128,4096]{1,0:T(8,128)(2,1)S(1)}, u32[]{:S(2)}, u32[]{:S(2)}) %collective-permute-start.17) | collective-permute-done | bytes 1048608 | tf_op jit(solution)/shard_map/ppermute | solution.py:122
  712.3 19.1 %collective-permute-done.18 = bf16[128,4096]{1,0:T(8,128)(2,1)} collective-permute-done((bf16[128,4096]{1,0:T(8,128)(2,1)}, bf16[128,4096]{1,0:T(8,128)(2,1)}, u32[]{:S(2)}, u32[]{:S(2)}) %collective-permute-start.18) | collective-permute-done | bytes 1048608 | tf_op jit(solution)/shard_map/ppermute | solution.py:122
  742.6 21.9 %all-gather.17.cloned.1.call-done = bf16[1024,1024]{1,0:T(8,128)(2,1)} async-done(((bf16[256,1024]{1,0:T(8,128)(2,1)}), bf16[1024,1024]{1,0:T(8,128)(2,1)}) %all-gather.17.cloned.1.call-update) | async-done | bytes 2097168 | tf_op jit(solution)/shard_map/all_gather | solution.py:314
  767.1 9.3 fusion.27
  776.4 13.2 %fusion.1 = (f32[2,2,1024]{2,1,0:T(2,128)S(1)}, f32[2,1024,1024,2]{2,1,3,0:T(8,128)}) fusion(f32[2,2,1024,1024]{2,3,1,0:T(8,128)} %get-tuple-element.196, f32[2,2,1024]{2,1,0:T(2,128)S(1)} %log_add_fusion, bf16[1024,2,64,1]{0,2,3,1:T(8,128)(2,1)S(1)} %bitcast.159, bf16[1024,2,2,64]{0,3,2,1:T(8,128)(2,1)S(1)} %bitcast.152), kind=kOutput, calls=%fused_computation.5 | convolution fusion | flops 549449728 | bytes 34373632 | tf_op jit(solution)/shard_map/while/body/eval_jaxpr/qkgd,skd->kgqs/dot_general | solution.py:328
  789.6 8.3 fusion.3
  812.8 71.8 %reduce-scatter.21.cloned.1.call-done = bf16[128,896]{1,0:T(8,128)(2,1)} async-done(((bf16[1024,896]{1,0:T(8,128)(2,1)}), bf16[128,896]{1,0:T(8,128)(2,1)}) %reduce-scatter.21.cloned.1.call-update) | async-done | bytes 229392
  893.3 20.0 %collective-permute-done.23 = bf16[128,4096]{1,0:T(8,128)(2,1)} collective-permute-done((bf16[128,4096]{1,0:T(8,128)(2,1)}, bf16[128,4096]{1,0:T(8,128)(2,1)}, u32[]{:S(2)}, u32[]{:S(2)}) %collective-permute-start.23) | collective-permute-done | bytes 1048608 | tf_op jit(solution)/shard_map/ppermute | solution.py:122
  922.9 16.4 %collective-permute-done.24 = bf16[128,4096]{1,0:T(8,128)(2,1)} collective-permute-done((bf16[128,4096]{1,0:T(8,128)(2,1)}, bf16[128,4096]{1,0:T(8,128)(2,1)}, u32[]{:S(2)}, u32[]{:S(2)}) %collective-permute-start.24) | collective-permute-done | bytes 1048608 | tf_op jit(solution)/shard_map/ppermute | solution.py:122
  (342 shorter events, 221.0 us)
Async XLA Ops:
  7.2 145.1 %all-gather.9.cloned.1.call-start = ((), (), s32[]{:S(2)}) async-start(), calls=%async_computation.7 | async-start | bytes 1769472 | tf_op jit(solution)/shard_map/all_gather | solution.py:162
  8.9 145.4 %all-gather.7.cloned.1.call-start = ((), (), s32[]{:S(2)}) async-start(), calls=%async_computation.6 | async-start | bytes 2621440 | tf_op jit(solution)/shard_map/all_gather | solution.py:161
  9.6 281.0 %all-gather.11.cloned.1.call-start = ((), (), s32[]{:S(2)}) async-start(), calls=%async_computation.8 | async-start | bytes 9437184 | tf_op jit(solution)/shard_map/all_gather | solution.py:176
  12.4 341.9 %reduce-scatter.13.cloned.1.call-start = ((), (), s32[]{:S(2)}) async-start(), calls=%async_computation.9 | async-start | bytes 2621440 | tf_op jit(solution)/shard_map/reduce_scatter | solution.py:244
  15.1 79.0 %collective-permute-start.2 = (bf16[128,4096]{1,0:T(8,128)(2,1)}, bf16[128,4096]{1,0:T(8,128)(2,1)S(1)}, u32[]{:S(2)}, u32[]{:S(2)}) collective-permute-start(bf16[128,4096]{1,0:T(8,128)(2,1)} %bitcast.138), channel_id=1, source_target_pairs={{0,4},{8,0},{16,8},{24,16},{28,24},{20,28},{12,20},{4,12},{1,5},{9... | collective-permute-start | bytes 3145736 | tf_op jit(solution)/shard_map/ppermute | solution.py:97
  20.6 73.5 %collective-permute-start = (bf16[128,4096]{1,0:T(8,128)(2,1)}, bf16[128,4096]{1,0:T(8,128)(2,1)S(1)}, u32[]{:S(2)}, u32[]{:S(2)}) collective-permute-start(bf16[128,4096]{1,0:T(8,128)(2,1)} %bitcast.139), channel_id=1, source_target_pairs={{0,8},{8,16},{16,24},{24,28},{28,20},{20,12},{12,4},{4,0},{1,9},{9... | collective-permute-start | bytes 3145736 | tf_op jit(solution)/shard_map/ppermute | solution.py:97
  94.1 57.2 %collective-permute-start.3 = (bf16[128,4096]{1,0:T(8,128)(2,1)S(1)}, bf16[128,4096]{1,0:T(8,128)(2,1)S(1)}, u32[]{:S(2)}, u32[]{:S(2)}) collective-permute-start(bf16[128,4096]{1,0:T(8,128)(2,1)S(1)} %collective-permute-done.2), channel_id=1, source_target_pairs={{0,4},{8,0},{16,8},{24,16},{28,24},{20,28},{12,20},{4,12},{1,5},{9... | collective-permute-start | bytes 3145736 | tf_op jit(solution)/shard_map/ppermute | solution.py:97
  94.2 58.1 %collective-permute-start.1 = (bf16[128,4096]{1,0:T(8,128)(2,1)S(1)}, bf16[128,4096]{1,0:T(8,128)(2,1)}, u32[]{:S(2)}, u32[]{:S(2)}) collective-permute-start(bf16[128,4096]{1,0:T(8,128)(2,1)S(1)} %collective-permute-done), channel_id=1, source_target_pairs={{0,8},{8,16},{16,24},{24,28},{28,20},{20,12},{12,4},{4,0},{1,9},{9... | collective-permute-start | bytes 3145736 | tf_op jit(solution)/shard_map/ppermute | solution.py:97
  152.3 39.2 %collective-permute-start.4 = (bf16[128,4096]{1,0:T(8,128)(2,1)}, bf16[128,4096]{1,0:T(8,128)(2,1)}, u32[]{:S(2)}, u32[]{:S(2)}) collective-permute-start(bf16[128,4096]{1,0:T(8,128)(2,1)} %collective-permute-done.1), channel_id=1, source_target_pairs={{0,8},{8,16},{16,24},{24,28},{28,20},{20,12},{12,4},{4,0},{1,9},{9... | collective-permute-start | bytes 3145736 | tf_op jit(solution)/shard_map/ppermute | solution.py:97
  152.3 51.9 %collective-permute-start.7 = (bf16[128,4096]{1,0:T(8,128)(2,1)}, bf16[128,4096]{1,0:T(8,128)(2,1)}, u32[]{:S(2)}, u32[]{:S(2)}) collective-permute-start(bf16[128,4096]{1,0:T(8,128)(2,1)} %copy-done.28), channel_id=1, source_target_pairs={{0,4},{8,0},{16,8},{24,16},{28,24},{20,28},{12,20},{4,12},{1,5},{9... | collective-permute-start | bytes 3145736 | tf_op jit(solution)/shard_map/ppermute | solution.py:97
  191.5 51.3 %collective-permute-start.5 = (bf16[128,4096]{1,0:T(8,128)(2,1)}, bf16[128,4096]{1,0:T(8,128)(2,1)}, u32[]{:S(2)}, u32[]{:S(2)}) collective-permute-start(bf16[128,4096]{1,0:T(8,128)(2,1)} %collective-permute-done.4), channel_id=1, source_target_pairs={{0,8},{8,16},{16,24},{24,28},{28,20},{20,12},{12,4},{4,0},{1,9},{9... | collective-permute-start | bytes 3145736 | tf_op jit(solution)/shard_map/ppermute | solution.py:97
  204.3 61.9 %collective-permute-start.8 = (bf16[128,4096]{1,0:T(8,128)(2,1)}, bf16[128,4096]{1,0:T(8,128)(2,1)}, u32[]{:S(2)}, u32[]{:S(2)}) collective-permute-start(bf16[128,4096]{1,0:T(8,128)(2,1)} %collective-permute-done.7), channel_id=1, source_target_pairs={{0,4},{8,0},{16,8},{24,16},{28,24},{20,28},{12,20},{4,12},{1,5},{9... | collective-permute-start | bytes 3145736 | tf_op jit(solution)/shard_map/ppermute | solution.py:97
  242.9 46.7 %collective-permute-start.6 = (bf16[128,4096]{1,0:T(8,128)(2,1)}, bf16[128,4096]{1,0:T(8,128)(2,1)}, u32[]{:S(2)}, u32[]{:S(2)}) collective-permute-start(bf16[128,4096]{1,0:T(8,128)(2,1)} %collective-permute-done.5), channel_id=1, source_target_pairs={{0,8},{8,16},{16,24},{24,28},{28,20},{20,12},{12,4},{4,0},{1,9},{9... | collective-permute-start | bytes 3145736 | tf_op jit(solution)/shard_map/ppermute | solution.py:97
  266.1 24.5 %collective-permute-start.9 = (bf16[128,4096]{1,0:T(8,128)(2,1)}, bf16[128,4096]{1,0:T(8,128)(2,1)}, u32[]{:S(2)}, u32[]{:S(2)}) collective-permute-start(bf16[128,4096]{1,0:T(8,128)(2,1)} %collective-permute-done.8), channel_id=1, source_target_pairs={{0,4},{8,0},{16,8},{24,16},{28,24},{20,28},{12,20},{4,12},{1,5},{9... | collective-permute-start | bytes 3145736 | tf_op jit(solution)/shard_map/ppermute | solution.py:97
  290.7 91.9 %all-gather.13.cloned.1.call-start = ((), (), s32[]{:S(2)}) async-start(), calls=%async_computation.10 | async-start | bytes 2621440 | tf_op jit(solution)/shard_map/all_gather | solution.py:185
  291.3 107.5 %all-gather.15.cloned.1.call-start = ((), (), s32[]{:S(2)}) async-start(), calls=%async_computation.11 | async-start | bytes 2621440 | tf_op jit(solution)/shard_map/all_gather | solution.py:250
  329.5 24.8 %collective-permute-start.11 = (bf16[128,4096]{1,0:T(8,128)(2,1)}, bf16[128,4096]{1,0:T(8,128)(2,1)S(1)}, u32[]{:S(2)}, u32[]{:S(2)}) collective-permute-start(bf16[128,4096]{1,0:T(8,128)(2,1)} %collective-permute-done.9), channel_id=1, source_target_pairs={{0,4},{8,0},{16,8},{24,16},{28,24},{20,28},{12,20},{4,12},{1,5},{9... | collective-permute-start | bytes 3145736 | tf_op jit(solution)/shard_map/ppermute | solution.py:97
  354.5 25.7 %collective-permute-start.13 = (bf16[128,4096]{1,0:T(8,128)(2,1)S(1)}, bf16[128,4096]{1,0:T(8,128)(2,1)}, u32[]{:S(2)}, u32[]{:S(2)}) collective-permute-start(bf16[128,4096]{1,0:T(8,128)(2,1)S(1)} %collective-permute-done.10), channel_id=1, source_target_pairs={{0,8},{8,16},{16,24},{24,28},{28,20},{20,12},{12,4},{4,0},{1,9},{9... | collective-permute-start | bytes 3145736 | tf_op jit(solution)/shard_map/ppermute | solution.py:97
  360.8 291.5 %reduce-scatter.19.cloned.1.call-start = ((), (), s32[]{:S(2)}) async-start(), calls=%async_computation.15 | async-start | bytes 9437184
  485.1 252.0 %reduce-scatter.15.cloned.1.call-start = ((), (), s32[]{:S(2)}) async-start(), calls=%async_computation.12 | async-start | bytes 5570560 | tf_op jit(solution)/shard_map/reduce_scatter | solution.py:294
  497.8 84.9 %collective-permute-start.14 = (bf16[128,4096]{1,0:T(8,128)(2,1)}, bf16[128,4096]{1,0:T(8,128)(2,1)}, u32[]{:S(2)}, u32[]{:S(2)}) collective-permute-start(bf16[128,4096]{1,0:T(8,128)(2,1)} %constant_dynamic-slice_fusion.1), channel_id=1, source_target_pairs={{0,8},{8,16},{16,24},{24,28},{28,20},{20,12},{12,4},{4,0},{1,9},{9... | collective-permute-start | bytes 3145736 | tf_op jit(solution)/shard_map/ppermute | solution.py:122
  512.9 71.7 %collective-permute-start.15 = (bf16[128,4096]{1,0:T(8,128)(2,1)}, bf16[128,4096]{1,0:T(8,128)(2,1)}, u32[]{:S(2)}, u32[]{:S(2)}) collective-permute-start(bf16[128,4096]{1,0:T(8,128)(2,1)} %constant_dynamic-slice_fusion), channel_id=1, source_target_pairs={{0,4},{8,0},{16,8},{24,16},{28,24},{20,28},{12,20},{4,12},{1,5},{9... | collective-permute-start | bytes 3145736 | tf_op jit(solution)/shard_map/ppermute | solution.py:122
  654.6 110.0 %all-gather.17.cloned.1.call-start = ((), (), s32[]{:S(2)}) async-start(), calls=%async_computation.13 | async-start | bytes 2621440 | tf_op jit(solution)/shard_map/all_gather | solution.py:314
  654.6 25.0 %collective-permute-start.16 = (bf16[128,4096]{1,0:T(8,128)(2,1)S(1)}, bf16[128,4096]{1,0:T(8,128)(2,1)S(1)}, u32[]{:S(2)}, u32[]{:S(2)}) collective-permute-start(bf16[128,4096]{1,0:T(8,128)(2,1)S(1)} %add_convert_fusion.12), channel_id=1, source_target_pairs={{0,8},{8,16},{16,24},{24,28},{28,20},{20,12},{12,4},{4,0},{1,9},{9... | collective-permute-start | bytes 3145736 | tf_op jit(solution)/shard_map/ppermute | solution.py:122
  654.8 26.7 %collective-permute-start.19 = (bf16[128,4096]{1,0:T(8,128)(2,1)S(1)}, bf16[128,4096]{1,0:T(8,128)(2,1)S(1)}, u32[]{:S(2)}, u32[]{:S(2)}) collective-permute-start(bf16[128,4096]{1,0:T(8,128)(2,1)S(1)} %add_convert_fusion.11), channel_id=1, source_target_pairs={{0,4},{8,0},{16,8},{24,16},{28,24},{20,28},{12,20},{4,12},{1,5},{9... | collective-permute-start | bytes 3145736 | tf_op jit(solution)/shard_map/ppermute | solution.py:122
  683.0 25.3 %collective-permute-start.20 = (bf16[128,4096]{1,0:T(8,128)(2,1)S(1)}, bf16[128,4096]{1,0:T(8,128)(2,1)S(1)}, u32[]{:S(2)}, u32[]{:S(2)}) collective-permute-start(bf16[128,4096]{1,0:T(8,128)(2,1)S(1)} %add_convert_fusion.7), channel_id=1, source_target_pairs={{0,4},{8,0},{16,8},{24,16},{28,24},{20,28},{12,20},{4,12},{1,5},{9... | collective-permute-start | bytes 3145736 | tf_op jit(solution)/shard_map/ppermute | solution.py:122
  742.3 142.3 %reduce-scatter.21.cloned.1.call-start = ((), (), s32[]{:S(2)}) async-start(), calls=%async_computation.16 | async-start | bytes 2064384
  810.7 138.7 %reduce-scatter.23.cloned.1.call-start = ((), (), s32[]{:S(2)}) async-start(), calls=%async_computation.17 | async-start | bytes 81920
  810.7 75.9 %collective-permute-start.22 = (bf16[128,4096]{1,0:T(8,128)(2,1)}, bf16[128,4096]{1,0:T(8,128)(2,1)}, u32[]{:S(2)}, u32[]{:S(2)}) collective-permute-start(bf16[128,4096]{1,0:T(8,128)(2,1)} %add_convert_fusion.8), channel_id=1, source_target_pairs={{0,8},{8,16},{16,24},{24,28},{28,20},{20,12},{12,4},{4,0},{1,9},{9... | collective-permute-start | bytes 3145736 | tf_op jit(solution)/shard_map/ppermute | solution.py:122
  812.3 78.0 %collective-permute-start.25 = (bf16[128,4096]{1,0:T(8,128)(2,1)}, bf16[128,4096]{1,0:T(8,128)(2,1)}, u32[]{:S(2)}, u32[]{:S(2)}) collective-permute-start(bf16[128,4096]{1,0:T(8,128)(2,1)} %add_convert_fusion.5), channel_id=1, source_target_pairs={{0,4},{8,0},{16,8},{24,16},{28,24},{20,28},{12,20},{4,12},{1,5},{9... | collective-permute-start | bytes 3145736 | tf_op jit(solution)/shard_map/ppermute | solution.py:122
  886.5 64.9 %reduce-scatter.17.cloned.1.call-start = ((), (), s32[]{:S(2)}) async-start(), calls=%async_computation.14 | async-start | bytes 2621440 | tf_op jit(solution)/shard_map/reduce_scatter | solution.py:368
  892.1 25.3 %collective-permute-start.26 = (bf16[128,4096]{1,0:T(8,128)(2,1)S(1)}, bf16[128,4096]{1,0:T(8,128)(2,1)S(1)}, u32[]{:S(2)}, u32[]{:S(2)}) collective-permute-start(bf16[128,4096]{1,0:T(8,128)(2,1)S(1)} %add_convert_fusion.2), channel_id=1, source_target_pairs={{0,4},{8,0},{16,8},{24,16},{28,24},{20,28},{12,20},{4,12},{1,5},{9... | collective-permute-start | bytes 3145736 | tf_op jit(solution)/shard_map/ppermute | solution.py:122
  (80 other events, 2740.9 us)
Sparse Core Ops, SparseCore 0:
  10.8 52.9 all-gather.8
  65.3 25.3 all-gather.6
  93.4 178.0 all-gather.10
  290.8 30.4 reduce-scatter.12
  322.7 22.5 all-gather.12
  360.9 20.2 all-gather.14
  485.2 167.0 reduce-scatter.18
  654.8 45.1 reduce-scatter.14
  742.4 22.1 all-gather.16
  810.8 73.7 reduce-scatter.20
  888.2 18.2 reduce-scatter.22
  909.0 31.3 reduce-scatter.16
